TPU v7x, 32 devices: a whole 2x2x4 slice. The times are simulated.
32 devices in a mesh: groups: 2 (over x), family: 16 (over z, y, core).
Axes of the slice: x: 2, y: 2, z: 4, core: 2. Of those that a mesh axis runs over, the one named last changes fastest.
Arguments:
- fraction: float32 [128, 32, 32, 128], P(('groups', 'family')), parts along dimension 0, may hold values from 0 to 1
- fraction_start: float32 [128, 32, 32, 128], P(('groups', 'family')), parts along dimension 0, may hold values from 0 to 1
- velocity: bfloat16 [128, 3, 32, 32, 128], P(('groups', 'family')), parts along dimension 0, may hold values from -12 to 12
- interface_flags: int32 [128, 32, 32, 128], P(('groups', 'family')), parts along dimension 0, may hold values 0 or 1
- block_links: int32 [64, 4, 3], P('family'), may hold values from 0 to 63, as said below
- deck_node: int32 [64, 32, 32], P('family'), may hold values from 0 to 2047
- mode_shapes: float32 [40, 2048], replicated, may hold values from -4 to 4
- mobility: float32 [40], replicated, may hold values from 0.3 to 3
Outputs:
- updated_fraction: float32 [128, 32, 32, 128], P(('groups', 'family')), parts along dimension 0
- deck_speed: float32 [128, 32, 32], P(('groups', 'family')), parts along dimension 0
There are 2 independent parts, one for each index of `groups`. A program takes and returns all parts, laid end to end along the dimension named above; an argument that names none is the same for every part. Nothing has to cross between parts.
Inputs may be any that keep to these rules, and one draw needn't show every extreme that they name: `block_links`: every lateral face is matched with exactly one face of a block on another device, both ways with the same flip code. The blocks of device d (blocks d * 4 to (d + 1) * 4 - 1) have their partners on 4 partner devices, each sharing exactly 4 matched face pairs with d; every partner device's index differs from d's in exactly one bit, a different bit for each partner. Faces are matched in no particular order. Entries are partner block, partner face 0 to 3, flip 0 or 1.
All inputs are finite; a program needn't handle non-finite values. Where the computation divides by a largest or mean magnitude, that divisor is 1e-20 or more. No bound on the sum of `interface_flags` on one device may be relied on, other than what follows from the above.
Results may differ from a plain program's by a relative error of at most 0.0003.
Values sent between devices are 32-bit elements; how exact they have to be, the bound alone decides.
No kernel may reach another device: no remote copies, remote signals or barrier semaphores. Data moves between devices by JAX's collectives and lax.ppermute only.
A program may use at most 256 MiB of HBM per device.

v0:
```python
import math

import jax
import jax.numpy as jnp
from jax import lax
from jax.sharding import PartitionSpec as P

CAP = 4


CFL_NUMBER = 0.4
SHARPEN = 2.0
DECK_GAIN = 0.15
EPSILON = 1e-06


def swapped(x, axis, stride):
    return lax.ppermute(x, axis, [(i, i ^ 1 << stride) for i in range(lax.axis_size(axis))])


def minmod(first, second):
    return 0.5 * (jnp.sign(first) + jnp.sign(second)) * jnp.minimum(jnp.abs(first), jnp.abs(second))


def upwind(far_left, left_cell, right_cell, far_right, face_speed):
    left_value = left_cell + 0.5 * minmod(left_cell - far_left, right_cell - left_cell)
    right_value = right_cell - 0.5 * minmod(right_cell - left_cell, far_right - right_cell)
    return jnp.maximum(face_speed, 0.0) * left_value + jnp.minimum(face_speed, 0.0) * right_value


def face_layers(fill, flow_field):
    first = jnp.stack([fill[:, 0], fill[:, 1], -flow_field[:, 0, 0]], 1)
    second = jnp.stack([fill[:, -1], fill[:, -2], flow_field[:, 0, -1]], 1)
    third = jnp.stack([fill[:, :, 0], fill[:, :, 1], -flow_field[:, 1, :, 0]], 1)
    fourth = jnp.stack([fill[:, :, -1], fill[:, :, -2], flow_field[:, 1, :, -1]], 1)
    return jnp.stack([first, second, third, fourth], 1)


def block_rate(fill, flow_field, ghosts, deck_value):
    padded = jnp.concatenate(
        [ghosts[0, 1][None], ghosts[0, 0][None], fill, ghosts[1, 0][None], ghosts[1, 1][None]], 0
    )
    speeds = jnp.concatenate([ghosts[0, 2][None], flow_field[0], -ghosts[1, 2][None]], 0)
    flux_i = upwind(
        padded[:-3], padded[1:-2], padded[2:-1], padded[3:], 0.5 * (speeds[:-1] + speeds[1:])
    )
    padded_j = jnp.concatenate(
        [
            ghosts[2, 1][:, None],
            ghosts[2, 0][:, None],
            fill,
            ghosts[3, 0][:, None],
            ghosts[3, 1][:, None],
        ],
        1,
    )
    speeds_j = jnp.concatenate([ghosts[2, 2][:, None], flow_field[1], -ghosts[3, 2][:, None]], 1)
    flux_j = upwind(
        padded_j[:, :-3],
        padded_j[:, 1:-2],
        padded_j[:, 2:-1],
        padded_j[:, 3:],
        0.5 * (speeds_j[:, :-1] + speeds_j[:, 1:]),
    )
    edged = jnp.concatenate([fill[:, :, :1], fill, fill[:, :, -1:]], 2)
    vertical = flow_field[2]
    inner = upwind(
        edged[:, :, :-3],
        edged[:, :, 1:-2],
        edged[:, :, 2:-1],
        edged[:, :, 3:],
        0.5 * (vertical[:, :, :-1] + vertical[:, :, 1:]),
    )
    bottom = jnp.zeros_like(fill[:, :, :1])
    top = deck_value[:, :, None] * fill[:, :, -1:]
    flux_k = jnp.concatenate([bottom, inner, top], 2)
    return -(
        flux_i[1:]
        - flux_i[:-1]
        + (flux_j[:, 1:] - flux_j[:, :-1])
        + (flux_k[:, :, 1:] - flux_k[:, :, :-1])
    )


def local(
    fraction,
    fraction_start,
    velocity,
    interface_flags,
    block_links,
    deck_node,
    mode_shapes,
    mobility,
):
    blocks = fraction.shape[0]
    extent = fraction.shape[1]
    height = fraction.shape[3]
    devices = lax.axis_size("family")
    face_count = 4 * blocks
    flow_field = velocity.astype(jnp.float32)
    layers = face_layers(fraction, flow_field).reshape(face_count, 3, extent, height)
    partner = block_links[:, :, 0].reshape(face_count)
    part_face = block_links[:, :, 1].reshape(face_count)
    flipped = block_links[:, :, 2].reshape(face_count)
    owner_dev = partner // blocks
    face_index = jnp.arange(face_count, dtype=jnp.int32)
    same_owner = owner_dev[:, None] == owner_dev[None, :]
    send_rank = jnp.sum(same_owner & (face_index[None, :] < face_index[:, None]), axis=1)
    sender_face = partner % blocks * 4 + part_face
    recv_rank = jnp.sum(same_owner & (sender_face[None, :] < sender_face[:, None]), axis=1)
    my_index = lax.axis_index("family")
    bit_total = devices.bit_length() - 1
    bit_list = list(range(bit_total))
    ghosts = jnp.zeros_like(layers)
    for bit in bit_list:
        peer = jnp.bitwise_xor(my_index, 1 << bit)
        chosen = owner_dev == peer
        slots = jnp.where(chosen, send_rank, CAP)
        outgoing = (
            jnp.zeros((CAP, 3, extent, height), jnp.float32).at[slots].set(layers, mode="drop")
        )
        received = swapped(outgoing, "family", bit)
        picked = received[jnp.minimum(recv_rank, CAP - 1)]
        ghosts = jnp.where(chosen[:, None, None, None], picked, ghosts)
    ghosts = jnp.where(flipped[:, None, None, None] == 1, ghosts[:, :, ::-1, :], ghosts)
    ghosts = ghosts.reshape(blocks, 4, 3, extent, height)
    top_fill = fraction[:, :, :, -1]
    top_vertical = flow_field[:, 2, :, :, -1]
    pressure = (top_fill * (1.0 + top_vertical * top_vertical)).reshape(-1)
    columns = jnp.take(mode_shapes, deck_node.reshape(-1), axis=1)
    local_force = jnp.dot(columns, pressure, precision=lax.Precision.HIGHEST)
    local_speed = jnp.max(jnp.abs(flow_field))
    force_sum = lax.psum(local_force, "family")
    speed_top = lax.pmax(local_speed, "family")
    scale = math.sqrt(mode_shapes.shape[1]) / (blocks * devices * extent * extent)
    modal_speed = mobility * (force_sum * scale)
    deck_speed = jnp.tanh(
        DECK_GAIN * jnp.dot(modal_speed, columns, precision=lax.Precision.HIGHEST)
    ).reshape(blocks, extent, extent)
    rates = jax.vmap(block_rate)(fraction, flow_field, ghosts, deck_speed)
    rates = rates + SHARPEN * interface_flags.astype(jnp.float32) * fraction * (1.0 - fraction) * (
        2.0 * fraction - 1.0
    )
    time_step = CFL_NUMBER / (speed_top + EPSILON)
    updated = 0.75 * fraction_start + 0.25 * (fraction + time_step * rates)
    return (updated, deck_speed)


def solution(mesh):
    in_specs = (
        P(("groups", "family"), None, None, None),
        P(("groups", "family"), None, None, None),
        P(("groups", "family"), None, None, None, None),
        P(("groups", "family"), None, None, None),
        P("family", None, None),
        P("family", None, None),
        P(),
        P(),
    )
    out_specs = (P(("groups", "family"), None, None, None), P(("groups", "family"), None, None))
    return jax.shard_map(local, mesh=mesh, in_specs=in_specs, out_specs=out_specs, check_vma=False)
```

profile of v0, /device:TPU:0, one launch (start us, length us, event | category | flops | bytes accessed | tf_op | source)
XLA Modules:
  0.0 446.0 jit_solution(16913090303083815118)
XLA Ops:
  4.2 17.8 %copy.362 = bf16[4,3,32,32,128]{3,2,4,1,0:T(8,128)(2,1)} copy(bf16[4,3,32,32,128]{4,3,2,1,0:T(8,128)(2,1)} %param.10) | data formatting | bytes 6291456 | tf_op args[2]
  23.5 7.8 %slice.227 = f32[4,1,32,1,128]{3,2,4,1,0:T(8,128)} slice(bf16[4,3,32,32,128]{3,2,4,1,0:T(8,128)(2,1)} %copy.362), slice={[0:4], [1:2], [0:32], [31:32], [0:128]} | slice | bytes 131072 | tf_op jit(solution)/shard_map/slice | solution.py:35
  32.1 9.2 %convert_element_type.12 = f32[4,3,32,32,128]{3,2,4,1,0:T(8,128)} convert(bf16[4,3,32,32,128]{3,2,4,1,0:T(8,128)(2,1)S(1)} %copy-done) | non-fusion elementwise | flops 1572864 | bytes 9437184 | tf_op jit(solution)/shard_map/convert_element_type | solution.py:100
  43.1 7.8 %slice_negate_fusion = f32[4,1,32,1,128]{3,2,4,1,0:T(8,128)} fusion(f32[4,3,32,32,128]{3,2,4,1,0:T(8,128)} %convert_element_type.12), kind=kLoop, calls=%fused_computation.45 | loop fusion | flops 16384 | bytes 131072 | tf_op jit(solution)/shard_map/neg | solution.py:34
  51.1 6.6 %copy.371 = f32[4,1,32,1,128]{4,2,0,3,1:T(8,128)S(1)} copy(f32[4,1,32,1,128]{3,2,4,1,0:T(8,128)} %slice.227) | data formatting | bytes 131072 | tf_op jit(solution)/shard_map/slice | solution.py:35
  57.7 6.5 %copy.367 = f32[4,1,32,1,128]{4,2,0,3,1:T(8,128)S(1)} copy(f32[4,1,32,1,128]{3,2,4,1,0:T(8,128)} %slice_negate_fusion) | data formatting | bytes 131072 | tf_op jit(solution)/shard_map/neg | solution.py:34
  66.5 3.4 scatter_fusion
  69.8 4.1 collective-permute-start
  74.6 3.3 scatter_fusion.1
  80.2 3.2 scatter_fusion.2
  86.9 7.7 %copy.412 = f32[4,32,32,128]{2,1,3,0:T(8,128)} copy(f32[4,32,32,128]{3,2,1,0:T(8,128)S(1)} %copy-done.1) | data formatting | bytes 4194304 | tf_op args[0]
  94.6 11.7 %abs_reduce_fusion = f32[]{:T(128)} fusion(bf16[4,3,32,32,128]{3,2,4,1,0:T(8,128)(2,1)} %copy.362), kind=kLoop, calls=%fused_computation.9 | loop fusion | flops 4718591 | bytes 3145732 | tf_op jit(solution)/shard_map/reduce_max | solution.py:132
  109.5 14.2 %gather_fusion.4 = f32[4096,40]{1,0:T(8,128)} fusion(f32[40,2048]{0,1:T(8,128)S(1)} %copy.406, s32[4096]{0:T(1024)S(1)} %broadcast_clamp_fusion), kind=kCustom, calls=%fused_computation.4 | custom fusion | bytes 1327104 | tf_op jit(solution)/shard_map/jit(_take)/gather | solution.py:130
  123.7 2.8 fusion.29
  126.6 30.0 %psum.7 = f32[40]{0:T(128)S(1)} all-reduce(f32[40]{0:T(128)S(1)} %fusion.29), channel_id=1, replica_groups=mesh['groups'=2,'family'=16] {'family'}, use_global_device_ids=true, to_apply=%region_8.9 | all-reduce | flops 40 | bytes 320 | tf_op jit(solution)/shard_map/psum | solution.py:133
  156.5 3.7 fusion.23
  161.6 17.6 %slice_bitcast_fusion = (f32[4,32,32,128]{2,1,3,0:T(8,128)}, f32[4,32,32,128]{2,1,3,0:T(8,128)}, f32[4,32,32,128]{2,1,3,0:T(8,128)}) fusion(f32[4,3,32,32,128]{3,2,4,1,0:T(8,128)} %convert_element_type.12), kind=kLoop, calls=%fused_computation.26 | loop fusion | bytes 12582912 | tf_op jit(solution)/shard_map/vmap()/squeeze | solution.py:66
  181.2 8.6 %copy.426 = f32[4,32,32,127]{2,1,3,0:T(8,128)} copy(f32[4,32,32,127]{3,2,1,0:T(8,128)} %pad_maximum_fusion.13) | data formatting | bytes 4161536
  189.8 7.5 %copy.361 = f32[4,32,32,128]{2,1,3,0:T(8,128)} copy(f32[4,32,32,128]{3,2,1,0:T(8,128)S(1)} %copy-done.2) | data formatting | bytes 4194304 | tf_op args[1]
  197.3 8.4 %copy.408 = s32[4,32,32,128]{2,1,3,0:T(8,128)} copy(s32[4,32,32,128]{3,2,1,0:T(8,128)} %param.11) | data formatting | bytes 4194304 | tf_op args[3]
  205.6 38.7 %pmax.7 = f32[]{:T(128)} all-reduce(f32[]{:T(128)} %abs_reduce_fusion), channel_id=1, replica_groups=mesh['groups'=2,'family'=16] {'family'}, use_global_device_ids=true, to_apply=%region_1.2 | all-reduce | flops 1 | bytes 8 | tf_op jit(solution)/shard_map/pmax | solution.py:134
  245.9 22.1 %multiply_add_fusion.1 = f32[4,32,32,127]{2,1,3,0:T(8,128)} fusion(f32[4,32,32,1]{2,1,3,0:T(8,128)S(1)} %slice.251, f32[4,32,32,128]{2,1,3,0:T(8,128)} %copy.412, f32[4,32,32,127]{2,1,3,0:T(8,128)} %copy.426, f32[4,32,32,128]{2,1,3,0:T(8,128)} %get-tuple-element.22), kind=kLoop, calls=%fused_computation.57 | loop fusion | flops 15085568 | bytes 52101120 | tf_op jit(solution)/shard_map/vmap()/add | solution.py:28
  277.9 7.5 %copy.389 = f32[4,32,1,128]{2,1,3,0:T(8,128)} copy(f32[4,32,1,128]{3,1,0,2:T(8,128)S(1)} %get-tuple-element.36) | data formatting | bytes 131072 | tf_op jit(solution)/shard_map/vmap()/broadcast_in_dim;vmap()/squeeze | solution.py:57
  285.3 7.5 %copy.390 = f32[4,32,1,128]{2,1,3,0:T(8,128)} copy(f32[4,32,1,128]{3,1,0,2:T(8,128)S(1)} %get-tuple-element.37) | data formatting | bytes 131072 | tf_op jit(solution)/shard_map/vmap()/neg | solution.py:57
  292.8 7.5 %copy.391 = f32[4,32,1,128]{2,1,3,0:T(8,128)} copy(f32[4,32,1,128]{3,1,0,2:T(8,128)S(1)} %get-tuple-element.38) | data formatting | bytes 131072 | tf_op jit(solution)/shard_map/vmap()/broadcast_in_dim;vmap()/squeeze | solution.py:50
  300.3 7.5 %copy.393 = f32[4,32,1,128]{2,1,3,0:T(8,128)} copy(f32[4,32,1,128]{3,1,0,2:T(8,128)S(1)} %get-tuple-element.39) | data formatting | bytes 131072 | tf_op jit(solution)/shard_map/vmap()/broadcast_in_dim;vmap()/squeeze | solution.py:49
  307.8 7.5 %copy.397 = f32[4,32,1,128]{2,1,3,0:T(8,128)} copy(f32[4,32,1,128]{3,1,0,2:T(8,128)S(1)} %get-tuple-element.40) | data formatting | bytes 131072 | tf_op jit(solution)/shard_map/vmap()/broadcast_in_dim;vmap()/squeeze | solution.py:52
  315.3 7.4 %copy.400 = f32[4,32,1,128]{2,1,3,0:T(8,128)} copy(f32[4,32,1,128]{3,1,0,2:T(8,128)S(1)} %get-tuple-element.41) | data formatting | bytes 131072 | tf_op jit(solution)/shard_map/vmap()/broadcast_in_dim;vmap()/squeeze | solution.py:53
  322.7 33.0 %fusion.6 = f32[4,33,32,128]{2,1,3,0:T(8,128)} fusion(f32[4,32,32,128]{2,1,3,0:T(8,128)} %copy.412, f32[4,1,32,128]{2,1,3,0:T(1,128)S(1)} %bitcast.139, f32[4,1,32,128]{2,1,3,0:T(1,128)S(1)} %bitcast.137, f32[4,1,32,128]{2,1,3,0:T(1,128)S(1)} %bitcast.140, f32[4,1,32,128]{2,1,3,0:T(1,128)S(1)} %bitcast.138, f32[4,1,32,128]{2,1,3,0:T(1,128)S(1)} %bitcast.141, ...), kind=kLoop, calls=%fused_computation.22 | loop fusion | flops 19464192 | bytes 6750208 | tf_op jit(solution)/shard_map/vmap()/add | solution.py:28
  355.8 51.4 %multiply_add_fusion = f32[4,32,33,128]{2,1,3,0:T(8,128)} fusion(f32[4,32,1,128]{2,1,3,0:T(8,128)} %copy.400, f32[4,32,1,128]{2,1,3,0:T(8,128)} %copy.397, f32[4,32,32,128]{2,1,3,0:T(8,128)} %copy.412, f32[4,32,1,128]{2,1,3,0:T(8,128)} %copy.391, f32[4,32,1,128]{2,1,3,0:T(8,128)} %copy.393, f32[4,32,1,128]{2,1,3,0:T(8,128)} %copy.390, ...), kind=kLoop, calls=%fused_computation.51 | loop fusion | flops 19464192 | bytes 6750208 | tf_op jit(solution)/shard_map/vmap()/add | solution.py:28
  407.2 30.8 %fusion.16 = f32[4,32,32,128]{2,1,3,0:T(8,128)} fusion(f32[4,32,32,128]{2,1,3,0:T(8,128)} %copy.412, f32[4,32,33,128]{2,1,3,0:T(8,128)} %multiply_add_fusion, f32[4,33,32,128]{2,1,3,0:T(8,128)} %fusion.6, f32[4,32,32,1]{2,1,3,0:T(8,128)S(1)} %bitcast_multiply_fusion, f32[4,32,32,127]{2,1,3,0:T(8,128)} %multiply_add_fusion.1, s32[4,32,32,128]{2,1,3,0:T(8,128)} %copy.408, ...), kind=kLoop, calls=%fused_computation.35 | loop fusion | flops 11010048 | bytes 18874372 | tf_op jit(solution)/shard_map/add | solution.py:145
  438.1 7.6 %copy.413 = f32[4,32,32,128]{3,2,1,0:T(8,128)} copy(f32[4,32,32,128]{2,1,3,0:T(8,128)} %fusion.16) | data formatting | bytes 4194304
  (84 shorter events, 33.7 us)
Async XLA Ops:
  23.5 8.6 %copy-start = (bf16[4,3,32,32,128]{3,2,4,1,0:T(8,128)(2,1)S(1)}, bf16[4,3,32,32,128]{3,2,4,1,0:T(8,128)(2,1)}, u32[]{:S(2)}) copy-start(bf16[4,3,32,32,128]{3,2,4,1,0:T(8,128)(2,1)} %copy.362) | copy-start | bytes 9437188
  51.1 14.6 %slice-start = ((f32[4,32,32,128]{3,2,1,0:T(8,128)}), f32[4,2,32,128]{3,2,1,0:T(8,128)S(1)}, s32[]{:S(2)}) async-start(f32[4,32,32,128]{3,2,1,0:T(8,128)} %param.8), calls=%async_computation | async-start | bytes 262144 | tf_op jit(solution)/shard_map/slice | solution.py:32
  64.3 22.5 %copy-start.4 = (s32[4,32,32]{2,1,0:T(8,128)S(1)}, s32[4,32,32]{2,1,0:T(8,128)}, u32[]{:S(2)}) copy-start(s32[4,32,32]{2,1,0:T(8,128)} %param.13) | copy-start | bytes 49156
  64.3 22.7 %copy-start.1 = (f32[4,32,32,128]{3,2,1,0:T(8,128)S(1)}, f32[4,32,32,128]{3,2,1,0:T(8,128)}, u32[]{:S(2)}) copy-start(f32[4,32,32,128]{3,2,1,0:T(8,128)} %param.8) | copy-start | bytes 6291460
  65.6 14.6 %copy-start.5 = (s32[16]{0:T(128)S(1)}, s32[16]{0:T(128)}, u32[]{:S(2)}) copy-start(s32[16]{0:T(128)} %get-tuple-element.45) | copy-start | bytes 196
  69.8 202.8 %collective-permute-start = (f32[4,3,32,128]{3,2,1,0:T(8,128)}, f32[4,3,32,128]{3,2,1,0:T(8,128)}, u32[]{:S(2)}, u32[]{:S(2)}) collective-permute-start(f32[4,3,32,128]{3,2,1,0:T(8,128)} %scatter_fusion), channel_id=1, source_target_pairs={{0,8},{1,9},{2,10},{3,11},{4,12},{5,13},{6,14},{7,15},{8,0},{9,1},... | collective-permute-start | bytes 589832 | tf_op jit(solution)/shard_map/ppermute | solution.py:18
  77.9 193.2 %collective-permute-start.1 = (f32[4,3,32,128]{3,2,1,0:T(8,128)}, f32[4,3,32,128]{3,2,1,0:T(8,128)}, u32[]{:S(2)}, u32[]{:S(2)}) collective-permute-start(f32[4,3,32,128]{3,2,1,0:T(8,128)} %scatter_fusion.1), channel_id=1, source_target_pairs={{0,4},{1,5},{2,6},{3,7},{4,0},{5,1},{6,2},{7,3},{8,12},{9,13},{10,... | collective-permute-start | bytes 589832 | tf_op jit(solution)/shard_map/ppermute | solution.py:18
  83.4 186.2 %collective-permute-start.2 = (f32[4,3,32,128]{3,2,1,0:T(8,128)}, f32[4,3,32,128]{3,2,1,0:T(8,128)}, u32[]{:S(2)}, u32[]{:S(2)}) collective-permute-start(f32[4,3,32,128]{3,2,1,0:T(8,128)} %scatter_fusion.2), channel_id=1, source_target_pairs={{0,2},{1,3},{2,0},{3,1},{4,6},{5,7},{6,4},{7,5},{8,10},{9,11},{10,... | collective-permute-start | bytes 589832 | tf_op jit(solution)/shard_map/ppermute | solution.py:18
  86.0 182.1 %collective-permute-start.3 = (f32[4,3,32,128]{3,2,1,0:T(8,128)S(1)}, f32[4,3,32,128]{3,2,1,0:T(8,128)}, u32[]{:S(2)}, u32[]{:S(2)}) collective-permute-start(f32[4,3,32,128]{3,2,1,0:T(8,128)S(1)} %scatter_fusion.3), channel_id=1, source_target_pairs={{0,1},{1,0},{2,3},{3,2},{4,5},{5,4},{6,7},{7,6},{8,9},{9,8},{10,11... | collective-permute-start | bytes 589832 | tf_op jit(solution)/shard_map/ppermute | solution.py:18
  94.6 61.9 %copy-start.7 = (f32[40]{0:T(128)S(1)}, f32[40]{0:T(128)}, u32[]{:S(2)}) copy-start(f32[40]{0:T(128)} %param.15) | copy-start | bytes 484
  161.6 17.7 %copy-start.6 = (s32[16]{0:T(128)S(1)}, s32[16]{0:T(128)}, u32[]{:S(2)}) copy-start(s32[16]{0:T(128)} %get-tuple-element.16) | copy-start | bytes 196
  181.2 8.6 %copy-start.2 = (f32[4,32,32,128]{3,2,1,0:T(8,128)S(1)}, f32[4,32,32,128]{3,2,1,0:T(8,128)}, u32[]{:S(2)}) copy-start(f32[4,32,32,128]{3,2,1,0:T(8,128)} %param.9) | copy-start | bytes 6291460
  189.8 54.6 %copy-start.3 = (f32[4,32,32,1]{2,1,0,3:T(8,128)S(1)}, f32[4,32,32,1]{2,1,0,3:T(8,128)}, u32[]{:S(2)}) copy-start(f32[4,32,32,1]{2,1,0,3:T(8,128)} %broadcast_in_dim_reshape.3) | copy-start | bytes 49156
where the time goes:
time: 455 us; the launch traced here: 446 us
  local copies, waits for them, and re-layouts  186 us (41%)
  other arithmetic  175 us (38%)
  blocking collectives  68.7 us (15%)
  starting transfers between devices  7.16 us (2%)
  matrix products  6.49 us (1%)
    add x3, other arithmetic, upwind(): jnp.maximum(face_speed, 0.0) * left_value  107 us
    unnamed x29, local copies, waits for them, and re-layouts  60.3 us
    pmax x1, blocking collectives, local(): speed_top = lax.pmax(local_speed, 'family')  38.7 us
    add x1, other arithmetic, local(): updated = 0.75 * fraction_start + 0.25 * (fraction + time_step * rates)  30.8 us
    psum x1, blocking collectives, local(): force_sum = lax.psum(local_force, 'family')  30 us
    squeeze x1, local copies, waits for them, and re-layouts, block_rate(): vertical = flow_field[2]  17.6 us
    slice x2, local copies, waits for them, and re-layouts, face_layers(): flow_field[:, 1, :, -1]  14.4 us
    gather x1, local copies, waits for them, and re-layouts, local(): columns = jnp.take(mode_shapes, deck_node.reshape(-1), axis=1)  14.2 us
  transfers between devices with their start and end apart: 4, of which 0 were waited for; matrix products, arithmetic and copies ran while one was open for 28% of the time, Pallas kernels for 0%

commit v1 on v0

v1 whole, which is shorter than its diff:
```python
import functools
import math

import jax
import jax.numpy as jnp
from jax import lax
from jax.experimental import pallas as pl
from jax.experimental.pallas import tpu as pltpu
from jax.sharding import PartitionSpec as P

CAP = 4
CFL_NUMBER = 0.4
SHARPEN = 2.0
DECK_GAIN = 0.15
EPSILON = 1e-06
LANES = 128
VMEM_LIMIT = 40 * 1024 * 1024


def swapped(x, axis, stride):
    return lax.ppermute(x, axis, [(i, i ^ 1 << stride) for i in range(lax.axis_size(axis))])


def limited(first, second):
    return jnp.maximum(jnp.minimum(second, jnp.maximum(first, 0.0)), jnp.minimum(first, 0.0))


def set_bits(x):
    x = x - ((x >> 1) & 0x5555)
    x = (x & 0x3333) + ((x >> 2) & 0x3333)
    x = (x + (x >> 4)) & 0x0F0F
    return (x + (x >> 8)) & 0x1F


def route(links, me, blocks, bits, count, mask, sent, got):
    for k in range(bits):
        count[k] = 0
        mask[k] = 0
        for s in range(CAP):
            sent[k * CAP + s] = 0
            got[k * CAP + s] = -1
    shift = blocks.bit_length() - 1
    found = []
    for face in range(4 * blocks):
        b, t = face // 4, face % 4
        partner = links[b, t, 0]
        differ = (partner >> shift) ^ me
        k = jnp.int32(0)
        for q in range(1, bits):
            k = k + (differ >= (1 << q)).astype(jnp.int32)
        r = count[k]
        count[k] = r + 1
        sent[k * CAP + r] = face
        source = (partner & (blocks - 1)) * 4 + links[b, t, 1]
        mask[k] = mask[k] | (jnp.int32(1) << source)
        found.append((k, source))
    for face, (k, source) in enumerate(found):
        rank = set_bits(mask[k] & ((jnp.int32(1) << source) - 1))
        got[k * CAP + rank] = 2 * face + links[face // 4, face % 4, 2]


def pack_kernel(dims, links, node_ref, shapes_ref, fill_hbm, vel_hbm, *rest):
    blocks, ext, height, bits = dims
    outs = rest[:bits]
    red_ref, got, fill, vel, edge, left, right, count, mask, sent, sems = rest[bits:]
    area = ext * ext
    fill_copies, vel_copies = [], []
    for b in range(blocks):
        fill_copies.append(pltpu.make_async_copy(fill_hbm.at[b], fill.at[b], sems.at[0, b]))
        vel_copies.append(pltpu.make_async_copy(vel_hbm.at[b], vel.at[b], sems.at[1, b]))
        fill_copies[b].start()
        vel_copies[b].start()
    route(links, lax.axis_index("family"), blocks, bits, count, mask, sent, got)
    lane = lax.broadcasted_iota(jnp.int32, (ext, height), 1)
    rows = fill.reshape(blocks * area, height)
    pressure = jnp.zeros((ext, height), jnp.float32)
    speed = jnp.zeros((ext, height), jnp.bfloat16)
    for b in range(blocks):
        fill_copies[b].wait()
        vel_copies[b].wait()
        for side in range(2):
            x = vel[b, 1, :, side * (ext - 8) : side * (ext - 8) + 8, :].astype(jnp.float32)
            edge[pl.ds((b * 2 + side) * ext * 8, ext * 8), :] = x.reshape(ext * 8, height)

        def step(i, carry):
            pressure, speed = carry
            up = vel[b, 2, i]
            speed = jnp.maximum(speed, jnp.abs(vel[b, 0, i]))
            speed = jnp.maximum(speed, jnp.abs(vel[b, 1, i]))
            speed = jnp.maximum(speed, jnp.abs(up))
            up = up.astype(jnp.float32)
            push = fill[b, i] * (1.0 + up * up)
            at = b * ext + i
            pressure = jnp.where(lane == at, pltpu.roll(push, at + 1, 1), pressure)
            return pressure, speed

        pressure, speed = lax.fori_loop(0, ext, step, (pressure, speed), unroll=4)
    for k in range(bits):
        for s in range(CAP):
            face = sent[k * CAP + s]
            b, t = face >> 2, face & 3
            side = t & 1
            sign = (2 * side - 1).astype(jnp.float32)
            near = side * (ext - 1)
            after = near + 1 - 2 * side

            @pl.when(t < 2)
            def _():
                outs[k][s, 0] = fill[b, near]
                outs[k][s, 1] = fill[b, after]
                outs[k][s, 2] = vel[b, 0, near].astype(jnp.float32) * sign

            @pl.when(t >= 2)
            def _():
                outs[k][s, 0] = rows[pl.ds(b * area + near, ext, stride=ext), :]
                outs[k][s, 1] = rows[pl.ds(b * area + after, ext, stride=ext), :]
                outs[k][s, 2] = edge[pl.ds((b * 2 + side) * ext * 8 + side * 7, ext, stride=8), :] * sign

    node = node_ref[...].T
    high, low = node >> 7, node & 127
    groups = shapes_ref.shape[1] // LANES
    part = pressure.astype(jnp.bfloat16)
    first = part.astype(jnp.float32)
    second = pressure - first
    high_at = lax.broadcasted_iota(jnp.int32, (groups, height), 0)
    low_at = lax.broadcasted_iota(jnp.int32, (LANES, height), 0)
    for j in range(ext):
        cols = pl.ds(j * height, height)
        same = high_at == high[j : j + 1]
        left[0:groups, cols] = jnp.where(same, first[j : j + 1], 0.0).astype(jnp.bfloat16)
        left[groups : 2 * groups, cols] = jnp.where(same, second[j : j + 1], 0.0).astype(jnp.bfloat16)
        right[:, cols] = jnp.where(low_at == low[j : j + 1], 1.0, 0.0).astype(jnp.bfloat16)
    nodal = lax.dot_general(left[...], right[...], (((1,), (1,)), ((), ())), preferred_element_type=jnp.float32)
    nodal = nodal[:groups] + nodal[groups:]
    lane8 = lax.broadcasted_iota(jnp.int32, (8, LANES), 1)
    tiles = shapes_ref.shape[0] // 8
    top = jnp.max(jnp.max(speed.astype(jnp.float32), axis=0, keepdims=True), axis=1, keepdims=True)
    red = jnp.where(lane8 == tiles, top, 0.0)
    for t in range(tiles):
        total = jnp.zeros((8, LANES), jnp.float32)
        for g in range(groups):
            total = total + shapes_ref[8 * t : 8 * t + 8, g * LANES : (g + 1) * LANES] * nodal[g : g + 1]
        red = jnp.where(lane8 == t, jnp.sum(total, axis=1, keepdims=True), red)
    red_ref[...] = red


def rates_kernel(dims, fill_hbm, start_hbm, vel_hbm, flag_hbm, base_ref, rate_ref, rim_ref, fill, start, vel, flag, edge, sems):
    blocks, ext, height, bits = dims
    area = ext * ext
    copies = []
    for b in range(blocks):
        group = [
            pltpu.make_async_copy(fill_hbm.at[b], fill.at[b], sems.at[0, b]),
            pltpu.make_async_copy(vel_hbm.at[b], vel.at[b], sems.at[1, b]),
            pltpu.make_async_copy(flag_hbm.at[b], flag.at[b], sems.at[2, b]),
            pltpu.make_async_copy(start_hbm.at[b], start.at[b], sems.at[3, b]),
        ]
        for c in group:
            c.start()
        copies.append(group)
    lane = lax.broadcasted_iota(jnp.int32, (ext, height), 1)
    row = lax.broadcasted_iota(jnp.int32, (ext, height), 0)
    last_lane = lane == height - 1
    open_row = (row >= 1) & (row <= ext - 3)
    rows = fill.reshape(blocks * area, height)

    def across(f, h, u, axis, size, cut, masked):
        step = jnp.where(cut, 0.0, pltpu.roll(h, size - 1, axis) - h) if masked else pltpu.roll(h, size - 1, axis) - h
        slope = limited(pltpu.roll(step, 1, axis), step)
        behind = f - slope
        v = u + pltpu.roll(u, size - 1, axis)
        v = jnp.where(cut, 0.0, v)
        flux = v * jnp.where(v > 0.0, f + slope, pltpu.roll(behind, size - 1, axis))
        return pltpu.roll(flux, 1, axis) - flux

    def own(b, i, f, h):
        rate = across(f, h, vel[b, 2, i].astype(jnp.float32), 1, height, last_lane, True)
        rate = rate + across(f, h, vel[b, 1, i].astype(jnp.float32), 0, ext, ~open_row, False)
        sharp = (2.0 * SHARPEN) * f * (1.0 - f) * (2.0 * f - 1.0)
        rate = rate + jnp.where(flag[b, i] != 0, sharp, 0.0)
        base_ref[b, i] = 0.75 * start[b, i] + 0.25 * f
        return rate

    for b in range(blocks):
        for c in copies[b]:
            c.wait()
        f0 = fill[b, 0]
        rate_ref[b, 0] = own(b, 0, f0, 0.5 * f0)
        f1 = fill[b, 1]
        h1 = 0.5 * f1
        rate1 = own(b, 1, f1, h1)
        f2 = fill[b, 2]
        h2 = 0.5 * f2
        step = h2 - h1
        ahead = f1 + limited(h1 - 0.5 * f0, step)

        def layer(i, carry):
            f, h, step_before, ahead, flux_before, u_before, rate_before = carry
            f_next = fill[b, i + 1]
            h_next = 0.5 * f_next
            step = h_next - h
            slope = limited(step_before, step)
            u = vel[b, 0, i].astype(jnp.float32)
            v = u_before + u
            flux = v * jnp.where(v > 0.0, ahead, f - slope)
            rate_ref[b, i - 1] = rate_before + (flux_before - flux)
            return f_next, h_next, step, f + slope, flux, u, own(b, i, f, h)

        carry = (f2, h2, step, ahead, jnp.zeros_like(f0), vel[b, 0, 1].astype(jnp.float32), rate1)
        carry = lax.fori_loop(2, ext - 1, layer, carry)
        f, h, _, _, flux, _, rate = carry
        rate_ref[b, ext - 2] = rate + flux
        rate_ref[b, ext - 1] = own(b, ext - 1, f, h)

        for side in range(2):
            x = vel[b, 1, :, side * (ext - 8) : side * (ext - 8) + 8, :].astype(jnp.float32)
            edge[pl.ds(side * ext * 8, ext * 8), :] = x.reshape(ext * 8, height)
        for t in range(4):
            side = t % 2
            sign = 1.0 - 2.0 * side
            at = [side * (ext - 1) + d * (1 - 2 * side) for d in range(3)]
            if t < 2:
                cells = [fill[b, i] for i in at]
                flows = [vel[b, 0, i].astype(jnp.float32) * sign for i in at[:2]]
            else:
                cells = [rows[pl.ds(b * area + j, ext, stride=ext), :] for j in at]
                flows = [edge[pl.ds(side * ext * 8 + j % 8, ext, stride=8), :] * sign for j in at[:2]]
            step = 0.5 * (cells[1] - cells[0])
            slope = limited(step, 0.5 * (cells[2] - cells[1]))
            rim_ref[4 * b + t, 0] = cells[0]
            rim_ref[4 * b + t, 1] = step
            rim_ref[4 * b + t, 2] = cells[1] - slope
            rim_ref[4 * b + t, 3] = flows[0]
            rim_ref[4 * b + t, 4] = flows[0] + flows[1]


def final_kernel(dims, devices, got, mobility_ref, node_ref, shapes_ref, red_ref, base_ref, rate_ref, rim_ref, fill_hbm, *rest):
    blocks, ext, height, bits = dims
    ghosts = rest[:bits]
    out_hbm, deck_ref, ghost, out, top_fill, sems, fsems = rest[bits:]
    area = ext * ext
    tiles = shapes_ref.shape[0] // 8
    groups = shapes_ref.shape[1] // LANES
    fill_copies = [pltpu.make_async_copy(fill_hbm.at[b], top_fill.at[b], fsems.at[b]) for b in range(blocks)]
    for c in fill_copies:
        c.start()
    turned = 7 - lax.broadcasted_iota(jnp.int32, (8, height), 0)
    for k in range(bits):
        for s in range(CAP):
            code = got[k * CAP + s]
            face, flip = code >> 1, code & 1

            @pl.when((code >= 0) & (flip == 0))
            def _():
                ghost[face] = ghosts[k][s]

            @pl.when((code >= 0) & (flip == 1))
            def _():
                for c in range(3):
                    for q in range(ext // 8):
                        x = ghosts[k][s, c, ext - 8 - 8 * q : ext - 8 * q, :]
                        ghost[face, c, 8 * q : 8 * q + 8, :] = jnp.take_along_axis(x, turned, axis=0)

    red = red_ref[...]
    time_step = CFL_NUMBER / (red[0:1, tiles : tiles + 1] + EPSILON)
    eighth = 0.125 * time_step
    scale = math.sqrt(shapes_ref.shape[1]) / (blocks * devices * area)
    lane8 = lax.broadcasted_iota(jnp.int32, (8, LANES), 1)
    sub8 = lax.broadcasted_iota(jnp.int32, (8, LANES), 0)
    mobility = mobility_ref[...]
    sums = [jnp.zeros((8, LANES), jnp.float32) for _ in range(groups)]
    width = mobility.shape[1]
    for t in range(tiles):
        pick = lax.broadcasted_iota(jnp.int32, (8, width), 1) == 8 * t + lax.broadcasted_iota(jnp.int32, (8, width), 0)
        gain = jnp.sum(jnp.where(pick, mobility, 0.0), axis=1, keepdims=True)
        speed = jnp.broadcast_to(gain * (red[:, t : t + 1] * scale), (8, LANES))
        for g in range(groups):
            sums[g] = sums[g] + shapes_ref[8 * t : 8 * t + 8, g * LANES : (g + 1) * LANES] * speed
    node = node_ref[...].T
    high, low = node >> 7, node & 127
    deck = jnp.zeros((ext, height), jnp.float32)
    for g in range(groups):
        line = jnp.broadcast_to(jnp.sum(sums[g], axis=0, keepdims=True), (8, LANES))
        values = [jnp.take_along_axis(line, low[8 * q : 8 * q + 8], axis=1) for q in range(ext // 8)]
        deck = jnp.where(high == g, jnp.concatenate(values, 0), deck)
    deck = jnp.tanh(DECK_GAIN * deck)
    deck_ref[...] = deck.T
    lane = lax.broadcasted_iota(jnp.int32, (ext, height), 1)
    last_lane = lane == height - 1
    rows = out.reshape(blocks * area, height)
    twice = 2.0 * eighth
    deck = deck * twice

    def apply(ghost_face, rim_face):
        g0, g1, gv = ghost[ghost_face, 0], ghost[ghost_face, 1], ghost[ghost_face, 2]
        c0, step1, behind1, u0, v1 = (rim_ref[rim_face, q] for q in range(5))
        step0 = 0.5 * (c0 - g0)
        ghost_slope = limited(step0, 0.5 * (g0 - g1))
        slope = limited(step0, step1)
        v0 = gv + u0
        flux0 = v0 * jnp.where(v0 > 0.0, g0 + ghost_slope, c0 - slope)
        flux1 = v1 * jnp.where(v1 > 0.0, c0 + slope, behind1)
        return eighth * (flux0 - flux1), eighth * flux1

    copies = []
    for b in range(blocks):
        fill_copies[b].wait()

        def layer(i, carry):
            at = b * ext + i
            lid = jnp.where(last_lane, pltpu.roll(deck, height - 1 - at, 1), 0.0)
            out[b, i] = base_ref[b, i] + eighth * rate_ref[b, i] - lid * top_fill[b, i]
            return carry

        lax.fori_loop(0, ext, layer, 0, unroll=4)
        for t in range(4):
            side = t % 2
            near = side * (ext - 1)
            after = near + 1 - 2 * side
            add0, add1 = apply(4 * b + t, 4 * b + t)
            for where, add in ((near, add0), (after, add1)):
                if t < 2:
                    out[b, where] = out[b, where] + add
                else:
                    line = pl.ds(b * area + where, ext, stride=ext)
                    rows[line, :] = rows[line, :] + add
        copy = pltpu.make_async_copy(out.at[b], out_hbm.at[b], sems.at[b])
        copy.start()
        copies.append(copy)
    for copy in copies:
        copy.wait()


def local(fraction, fraction_start, velocity, interface_flags, block_links, deck_node, mode_shapes, mobility):
    blocks, ext, _, height = fraction.shape
    devices = lax.axis_size("family")
    bits = devices.bit_length() - 1
    modes, nodes = mode_shapes.shape
    faces = 4 * blocks
    dims = (blocks, ext, height, bits)
    f32 = jnp.float32
    vmem = pl.BlockSpec(memory_space=pltpu.VMEM)
    smem = pl.BlockSpec(memory_space=pltpu.SMEM)
    hbm = pl.BlockSpec(memory_space=pl.ANY)
    params = pltpu.CompilerParams(vmem_limit_bytes=VMEM_LIMIT)
    flat_node = deck_node.reshape(blocks * ext, ext)
    packed = pl.pallas_call(
        functools.partial(pack_kernel, dims),
        out_shape=[jax.ShapeDtypeStruct((CAP, 3, ext, height), f32)] * bits
        + [jax.ShapeDtypeStruct((8, LANES), f32), jax.ShapeDtypeStruct((bits * CAP,), jnp.int32)],
        in_specs=[smem, vmem, vmem, hbm, hbm],
        out_specs=[vmem] * (bits + 1) + [smem],
        scratch_shapes=[
            pltpu.VMEM((blocks, ext, ext, height), f32),
            pltpu.VMEM((blocks, 3, ext, ext, height), jnp.bfloat16),
            pltpu.VMEM((blocks * 2 * ext * 8, height), f32),
            pltpu.VMEM((2 * nodes // LANES, ext * height), jnp.bfloat16),
            pltpu.VMEM((LANES, ext * height), jnp.bfloat16),
            pltpu.SMEM((bits,), jnp.int32),
            pltpu.SMEM((bits,), jnp.int32),
            pltpu.SMEM((bits * CAP,), jnp.int32),
            pltpu.SemaphoreType.DMA((2, blocks)),
        ],
        compiler_params=params,
        name="pack",
    )(block_links, flat_node, mode_shapes, fraction, velocity)
    outgoing, red, got = packed[:bits], packed[bits], packed[bits + 1]
    received = [None] * bits
    for k in reversed(range(bits)):
        received[k] = swapped(outgoing[k], "family", k)
    is_top = lax.broadcasted_iota(jnp.int32, red.shape, 1) == modes // 8
    for k in range(bits):
        other = swapped(red, "family", k)
        red = jnp.where(is_top, jnp.maximum(red, other), red + other)
    base, rate, rim = pl.pallas_call(
        functools.partial(rates_kernel, dims),
        out_shape=[
            jax.ShapeDtypeStruct(fraction.shape, f32),
            jax.ShapeDtypeStruct(fraction.shape, f32),
            jax.ShapeDtypeStruct((faces, 5, ext, height), f32),
        ],
        in_specs=[hbm] * 4,
        out_specs=[vmem] * 3,
        scratch_shapes=[
            pltpu.VMEM((blocks, ext, ext, height), f32),
            pltpu.VMEM((blocks, ext, ext, height), f32),
            pltpu.VMEM((blocks, 3, ext, ext, height), jnp.bfloat16),
            pltpu.VMEM((blocks, ext, ext, height), jnp.int32),
            pltpu.VMEM((2 * ext * 8, height), f32),
            pltpu.SemaphoreType.DMA((4, blocks)),
        ],
        compiler_params=params,
        cost_estimate=pl.CostEstimate(flops=80 * fraction.size, bytes_accessed=20 * fraction.size, transcendentals=0),
        name="rates",
    )(fraction, fraction_start, velocity, interface_flags)
    updated, deck = pl.pallas_call(
        functools.partial(final_kernel, dims, devices),
        out_shape=[
            jax.ShapeDtypeStruct(fraction.shape, f32),
            jax.ShapeDtypeStruct((blocks * ext, ext), f32),
        ],
        in_specs=[smem] + [vmem] * 7 + [hbm] + [vmem] * bits,
        out_specs=[hbm, vmem],
        scratch_shapes=[
            pltpu.VMEM((faces, 3, ext, height), f32),
            pltpu.VMEM((blocks, ext, ext, height), f32),
            pltpu.VMEM((blocks, ext, ext, height), f32),
            pltpu.SemaphoreType.DMA((blocks,)),
            pltpu.SemaphoreType.DMA((blocks,)),
        ],
        compiler_params=params,
        name="finish",
    )(got, mobility.reshape(1, modes), flat_node, mode_shapes, red, base, rate, rim, fraction, *received)
    return updated, deck.reshape(blocks, ext, ext)


def solution(mesh):
    in_specs = (
        P(("groups", "family"), None, None, None),
        P(("groups", "family"), None, None, None),
        P(("groups", "family"), None, None, None, None),
        P(("groups", "family"), None, None, None),
        P("family", None, None),
        P("family", None, None),
        P(),
        P(),
    )
    out_specs = (P(("groups", "family"), None, None, None), P(("groups", "family"), None, None))
    return jax.shard_map(local, mesh=mesh, in_specs=in_specs, out_specs=out_specs, check_vma=False)
```

time: 455 us -> 70.7 us (0.16); the launches traced: 446 us -> 70.4 us
  local copies, waits for them, and re-layouts: 186 us -> 7.7 us
  other arithmetic: 175 us -> 0.02 us
  blocking collectives: 68.7 us -> 0 us
  Pallas kernels: 0 us -> 49.2 us
  matrix products: 6.49 us -> 0 us
    add x6 -> x0, other arithmetic: 138 us -> none  [the longest x3 107 us: upwind(): jnp.maximum(face_speed, 0.0) * left_value]
    squeeze x7 -> x0, local copies, waits for them, and re-layouts: 55.1 us -> none  [the longest x1 17.6 us: block_rate(): vertical = flow_field[2]]
    unnamed x29 -> x21, local copies, waits for them, and re-layouts: 60.3 us -> 7.7 us
    pallas_call x0 -> x3, Pallas kernels: none -> 49.2 us  [the longest x1 36.9 us: local(): pl.pallas_call(functools.partial(rates_kernel, dims), out_shape=[jax.Shap...]
    pmax x1 -> x0, blocking collectives: 38.7 us -> none  [local(): speed_top = lax.pmax(local_speed, 'family')]
    psum x1 -> x0, blocking collectives: 30 us -> none  [local(): force_sum = lax.psum(local_force, 'family')]
    gather x5 -> x0, local copies, waits for them, and re-layouts: 21.2 us -> none  [the longest x1 14.2 us: local(): columns = jnp.take(mode_shapes, deck_node.reshape(-1), axis=1)]
    slice x9 -> x0, local copies, waits for them, and re-layouts: 20.1 us -> none  [the longest x2 14.4 us: face_layers(): flow_field[:, 1, :, -1]]
  transfers between devices with their start and end apart: 4 -> 8, of which waited for: 0 -> 2; matrix products, arithmetic and copies ran while one was open for 28% -> 0% of each run, Pallas kernels for 0% -> 52%
where the time goes in v1:
time: 70.7 us; the launch traced here: 70.4 us
  Pallas kernels  49.2 us (70%)
  starting transfers between devices  10.4 us (15%)
  local copies, waits for them, and re-layouts  7.7 us (11%)
  waiting for transfers between devices  2.42 us (3%)
  between operations  0.73 us (1%)
    pallas_call x1, Pallas kernels, local(): pl.pallas_call(functools.partial(rates_kernel, dims), out_shape=[jax.Shap...  36.9 us
    ppermute x8, starting transfers between devices, swapped(): lax.ppermute(x, axis, [(i, i ^ 1 << stride) for i in range(lax.axis_size(...  10.4 us
    unnamed x21, local copies, waits for them, and re-layouts  7.7 us
    pallas_call x1, Pallas kernels, local(): pl.pallas_call(functools.partial(final_kernel, dims, devices), out_shape=...  6.48 us
    pallas_call x1, Pallas kernels, local(): pl.pallas_call(functools.partial(pack_kernel, dims), out_shape=[jax.Shape...  5.8 us
    ppermute x8, waiting for transfers between devices, swapped(): lax.ppermute(x, axis, [(i, i ^ 1 << stride) for i in range(lax.axis_size(...  2.42 us
  transfers between devices with their start and end apart: 8, of which 2 were waited for; matrix products, arithmetic and copies ran while one was open for 0% of the time, Pallas kernels for 52%

profile of v1, /device:TPU:0, one launch (start us, length us, event | category | flops | bytes accessed | tf_op | source)
XLA Modules:
  0.0 70.4 jit_solution(16916706357676706184)
XLA Ops:
  0.6 0.8 %copy.10.links = s32[4,4,3]{2,1,0:T(4,128)S(1)} copy(s32[4,4,3]{1,0,2:T(4,128)} %param.12) | data formatting | bytes 384 | tf_op args[4]
  1.4 0.0 copy-start
  1.4 1.6 %copy-done = f32[4,32,32,128]{3,2,1,0:T(8,128)S(1)} copy-done((f32[4,32,32,128]{3,2,1,0:T(8,128)S(1)}, f32[4,32,32,128]{3,2,1,0:T(8,128)}, u32[]{:S(2)}) %copy-start) | copy-done | bytes 2097176
  3.0 0.0 copy-start.2
  3.0 1.9 %copy-done.2 = bf16[4,3,32,32,128]{4,3,2,1,0:T(8,128)(2,1)S(1)} copy-done((bf16[4,3,32,32,128]{4,3,2,1,0:T(8,128)(2,1)S(1)}, bf16[4,3,32,32,128]{4,3,2,1,0:T(8,128)(2,1)}, u32[]{:S(2)}) %copy-start.2) | copy-done | bytes 3145752
  4.9 1.0 %copy-done.5 = f32[40,2048]{1,0:T(8,128)S(1)} copy-done((f32[40,2048]{1,0:T(8,128)S(1)}, f32[40,2048]{1,0:T(8,128)}, u32[]{:S(2)}) %copy-start.5) | copy-done | bytes 327704
  5.9 0.8 %copy-done.7 = s32[4,32,32]{2,1,0:T(8,128)S(1)} copy-done((s32[4,32,32]{2,1,0:T(8,128)S(1)}, s32[4,32,32]{2,1,0:T(8,128)}, u32[]{:S(2)}) %copy-start.7) | copy-done | bytes 16408
  6.7 5.8 %pack.1 = (f32[4,3,32,128]{3,2,1,0:T(8,128)S(1)}, f32[4,3,32,128]{3,2,1,0:T(8,128)S(1)}, f32[4,3,32,128]{3,2,1,0:T(8,128)S(1)}, f32[4,3,32,128]{3,2,1,0:T(8,128)...) custom-call(s32[4,4,3]{2,1,0:T(4,128)S(1)} %copy.10.links, s32[128,32]{1,0:T(8,128)S(1)} %bitcast.3, f32[40,2048]{1,0:T(8,128)S(1)} %copy-done.5, ...), custom_call_target="tpu_custom_call" | custom-call | tf_op jit(solution)/shard_map/pack/pallas_call | solution.py:347
  12.5 0.5 collective-permute-start
  13.1 0.8 %collective-permute-done = f32[8,128]{1,0:T(8,128)S(1)} collective-permute-done((f32[8,128]{1,0:T(8,128)S(1)}, f32[8,128]{1,0:T(8,128)S(1)}, u32[]{:S(2)}, u32[]{:S(2)}) %collective-permute-start) | collective-permute-done | bytes 4128 | tf_op jit(solution)/shard_map/ppermute | solution.py:21
  13.9 2.9 %collective-permute-start.1 = (f32[8,128]{1,0:T(8,128)S(1)}, f32[8,128]{1,0:T(8,128)S(1)}, u32[]{:S(2)}, u32[]{:S(2)}) collective-permute-start(f32[8,128]{1,0:T(8,128)S(1)} %add_select_fusion.3), channel_id=1, source_target_pairs={{0,2},{1,3},{2,0},{3,1},{4,6},{5,7},{6,4},{7,5},{8,10},{9,11},{10,... | collective-permute-start | bytes 12296 | tf_op jit(solution)/shard_map/ppermute | solution.py:21
  16.7 1.6 %collective-permute-done.1 = f32[8,128]{1,0:T(8,128)S(1)} collective-permute-done((f32[8,128]{1,0:T(8,128)S(1)}, f32[8,128]{1,0:T(8,128)S(1)}, u32[]{:S(2)}, u32[]{:S(2)}) %collective-permute-start.1) | collective-permute-done | bytes 4128 | tf_op jit(solution)/shard_map/ppermute | solution.py:21
  18.3 2.1 %collective-permute-start.2 = (f32[8,128]{1,0:T(8,128)S(1)}, f32[8,128]{1,0:T(8,128)S(1)}, u32[]{:S(2)}, u32[]{:S(2)}) collective-permute-start(f32[8,128]{1,0:T(8,128)S(1)} %add_select_fusion.2), channel_id=1, source_target_pairs={{0,4},{1,5},{2,6},{3,7},{4,0},{5,1},{6,2},{7,3},{8,12},{9,13},{10,... | collective-permute-start | bytes 12296 | tf_op jit(solution)/shard_map/ppermute | solution.py:21
  20.4 0.0 collective-permute-start.4
  20.4 1.5 %collective-permute-start.5 = (f32[4,3,32,128]{3,2,1,0:T(8,128)S(1)}, f32[4,3,32,128]{3,2,1,0:T(8,128)S(1)}, u32[]{:S(2)}, u32[]{:S(2)}) collective-permute-start(f32[4,3,32,128]{3,2,1,0:T(8,128)S(1)} %get-tuple-element.19), channel_id=1, source_target_pairs={{0,2},{1,3},{2,0},{3,1},{4,6},{5,7},{6,4},{7,5},{8,10},{9,11},{10,... | collective-permute-start | bytes 589832 | tf_op jit(solution)/shard_map/ppermute | solution.py:21
  21.9 0.4 collective-permute-start.6
  22.4 0.0 collective-permute-done.2
  22.4 2.6 %collective-permute-start.3 = (f32[8,128]{1,0:T(8,128)S(1)}, f32[8,128]{1,0:T(8,128)S(1)}, u32[]{:S(2)}, u32[]{:S(2)}) collective-permute-start(f32[8,128]{1,0:T(8,128)S(1)} %add_select_fusion.1), channel_id=1, source_target_pairs={{0,8},{1,9},{2,10},{3,11},{4,12},{5,13},{6,14},{7,15},{8,0},{9,1},... | collective-permute-start | bytes 12296 | tf_op jit(solution)/shard_map/ppermute | solution.py:21
  25.0 0.3 collective-permute-start.7
  25.3 0.0 copy-done.1
  25.3 0.0 copy-done.3
  25.3 1.6 %copy-done.4 = s32[4,32,32,128]{3,2,1,0:T(8,128)S(1)} copy-done((s32[4,32,32,128]{3,2,1,0:T(8,128)S(1)}, s32[4,32,32,128]{3,2,1,0:T(8,128)}, u32[]{:S(2)}) %copy-start.4) | copy-done | bytes 2097176
  26.9 36.9 %rates.1 = (f32[4,32,32,128]{3,2,1,0:T(8,128)S(1)}, f32[4,32,32,128]{3,2,1,0:T(8,128)S(1)}, f32[16,5,32,128]{3,2,1,0:T(8,128)S(1)}) custom-call(f32[4,32,32,128]{3,2,1,0:T(8,128)S(1)} %copy-done.1, f32[4,32,32,128]{3,2,1,0:T(8,128)S(1)} %copy-done.3, bf16[4,3,32,32,128]{4,3,2,1,0:T(8,128)(2,1)} %vel_hbm.3, s32[4,32,32,128]{3,2,1,0:T(8,128)S(1)} %copy-done.4), custom_call_target="tpu_custom_call" | custom-call | flops 41943040 | bytes 10485760 | tf_op jit(solution)/shard_map/rates/pallas_call | solution.py:375
  63.8 0.0 collective-permute-done.3
  63.9 0.0 collective-permute-done.4.rest_0_
  63.9 0.0 collective-permute-done.5.rest_1_
  63.9 0.0 collective-permute-done.6.rest_2_
  63.9 0.0 collective-permute-done.7.rest_3_
  63.9 0.0 copy-done.6
  63.9 0.0 copy-done.8
  63.9 0.0 copy-done.9
  63.9 6.5 %finish.1 = (f32[4,32,32,128]{3,2,1,0:T(8,128)}, f32[128,32]{1,0:T(8,128)}) custom-call(s32[16]{0:T(128)S(1)} %get-tuple-element.13.got, f32[1,40]{1,0:T(1,128)S(1)} %bitcast.5, s32[128,32]{1,0:T(8,128)S(1)} %bitcast.4, f32[40,2048]{1,0:T(8,128)S(1)} %copy-done.6, f32[8,128]{1,0:T(8,128)S(1)} %add_select_fusion.red_ref, ...), custom_call_target="tpu_custom_call" | custom-call | tf_op jit(solution)/shard_map/finish/pallas_call | solution.py:396
  (13 shorter events, 0.0 us)
Async XLA Ops:
  1.4 1.6 %copy-start = (f32[4,32,32,128]{3,2,1,0:T(8,128)S(1)}, f32[4,32,32,128]{3,2,1,0:T(8,128)}, u32[]{:S(2)}) copy-start(f32[4,32,32,128]{3,2,1,0:T(8,128)} %fill_hbm.5) | copy-start | bytes 6291460
  3.0 1.9 %copy-start.2 = (bf16[4,3,32,32,128]{4,3,2,1,0:T(8,128)(2,1)S(1)}, bf16[4,3,32,32,128]{4,3,2,1,0:T(8,128)(2,1)}, u32[]{:S(2)}) copy-start(bf16[4,3,32,32,128]{4,3,2,1,0:T(8,128)(2,1)} %vel_hbm.3) | copy-start | bytes 9437188
  4.9 1.0 %copy-start.5 = (f32[40,2048]{1,0:T(8,128)S(1)}, f32[40,2048]{1,0:T(8,128)}, u32[]{:S(2)}) copy-start(f32[40,2048]{1,0:T(8,128)} %shapes_ref.3) | copy-start | bytes 983044
  5.9 0.8 %copy-start.7 = (s32[4,32,32]{2,1,0:T(8,128)S(1)}, s32[4,32,32]{2,1,0:T(8,128)}, u32[]{:S(2)}) copy-start(s32[4,32,32]{2,1,0:T(8,128)} %param.13) | copy-start | bytes 49156
  6.7 18.6 %copy-start.1 = (f32[4,32,32,128]{3,2,1,0:T(8,128)S(1)}, f32[4,32,32,128]{3,2,1,0:T(8,128)}, u32[]{:S(2)}) copy-start(f32[4,32,32,128]{3,2,1,0:T(8,128)} %fill_hbm.5) | copy-start | bytes 6291460
  6.7 18.6 %copy-start.3 = (f32[4,32,32,128]{3,2,1,0:T(8,128)S(1)}, f32[4,32,32,128]{3,2,1,0:T(8,128)}, u32[]{:S(2)}) copy-start(f32[4,32,32,128]{3,2,1,0:T(8,128)} %start_hbm.1) | copy-start | bytes 6291460
  12.5 1.3 %collective-permute-start = (f32[8,128]{1,0:T(8,128)S(1)}, f32[8,128]{1,0:T(8,128)S(1)}, u32[]{:S(2)}, u32[]{:S(2)}) collective-permute-start(f32[8,128]{1,0:T(8,128)S(1)} %get-tuple-element.14), channel_id=1, source_target_pairs={{0,1},{1,0},{2,3},{3,2},{4,5},{5,4},{6,7},{7,6},{8,9},{9,8},{10,11... | collective-permute-start | bytes 12296 | tf_op jit(solution)/shard_map/ppermute | solution.py:21
  13.9 4.4 %collective-permute-start.1 = (f32[8,128]{1,0:T(8,128)S(1)}, f32[8,128]{1,0:T(8,128)S(1)}, u32[]{:S(2)}, u32[]{:S(2)}) collective-permute-start(f32[8,128]{1,0:T(8,128)S(1)} %add_select_fusion.3), channel_id=1, source_target_pairs={{0,2},{1,3},{2,0},{3,1},{4,6},{5,7},{6,4},{7,5},{8,10},{9,11},{10,... | collective-permute-start | bytes 12296 | tf_op jit(solution)/shard_map/ppermute | solution.py:21
  18.3 4.1 %collective-permute-start.2 = (f32[8,128]{1,0:T(8,128)S(1)}, f32[8,128]{1,0:T(8,128)S(1)}, u32[]{:S(2)}, u32[]{:S(2)}) collective-permute-start(f32[8,128]{1,0:T(8,128)S(1)} %add_select_fusion.2), channel_id=1, source_target_pairs={{0,4},{1,5},{2,6},{3,7},{4,0},{5,1},{6,2},{7,3},{8,12},{9,13},{10,... | collective-permute-start | bytes 12296 | tf_op jit(solution)/shard_map/ppermute | solution.py:21
  20.4 43.5 %collective-permute-start.4 = (f32[4,3,32,128]{3,2,1,0:T(8,128)S(1)}, f32[4,3,32,128]{3,2,1,0:T(8,128)S(1)}, u32[]{:S(2)}, u32[]{:S(2)}) collective-permute-start(f32[4,3,32,128]{3,2,1,0:T(8,128)S(1)} %get-tuple-element.18), channel_id=1, source_target_pairs={{0,1},{1,0},{2,3},{3,2},{4,5},{5,4},{6,7},{7,6},{8,9},{9,8},{10,11... | collective-permute-start | bytes 589832 | tf_op jit(solution)/shard_map/ppermute | solution.py:21
  20.4 43.5 %collective-permute-start.5 = (f32[4,3,32,128]{3,2,1,0:T(8,128)S(1)}, f32[4,3,32,128]{3,2,1,0:T(8,128)S(1)}, u32[]{:S(2)}, u32[]{:S(2)}) collective-permute-start(f32[4,3,32,128]{3,2,1,0:T(8,128)S(1)} %get-tuple-element.19), channel_id=1, source_target_pairs={{0,2},{1,3},{2,0},{3,1},{4,6},{5,7},{6,4},{7,5},{8,10},{9,11},{10,... | collective-permute-start | bytes 589832 | tf_op jit(solution)/shard_map/ppermute | solution.py:21
  21.9 42.0 %collective-permute-start.6 = (f32[4,3,32,128]{3,2,1,0:T(8,128)S(1)}, f32[4,3,32,128]{3,2,1,0:T(8,128)S(1)}, u32[]{:S(2)}, u32[]{:S(2)}) collective-permute-start(f32[4,3,32,128]{3,2,1,0:T(8,128)S(1)} %get-tuple-element.20), channel_id=1, source_target_pairs={{0,4},{1,5},{2,6},{3,7},{4,0},{5,1},{6,2},{7,3},{8,12},{9,13},{10,... | collective-permute-start | bytes 589832 | tf_op jit(solution)/shard_map/ppermute | solution.py:21
  22.4 41.5 %collective-permute-start.3 = (f32[8,128]{1,0:T(8,128)S(1)}, f32[8,128]{1,0:T(8,128)S(1)}, u32[]{:S(2)}, u32[]{:S(2)}) collective-permute-start(f32[8,128]{1,0:T(8,128)S(1)} %add_select_fusion.1), channel_id=1, source_target_pairs={{0,8},{1,9},{2,10},{3,11},{4,12},{5,13},{6,14},{7,15},{8,0},{9,1},... | collective-permute-start | bytes 12296 | tf_op jit(solution)/shard_map/ppermute | solution.py:21
  25.0 38.9 %collective-permute-start.7 = (f32[4,3,32,128]{3,2,1,0:T(8,128)S(1)}, f32[4,3,32,128]{3,2,1,0:T(8,128)S(1)}, u32[]{:S(2)}, u32[]{:S(2)}) collective-permute-start(f32[4,3,32,128]{3,2,1,0:T(8,128)S(1)} %get-tuple-element.21), channel_id=1, source_target_pairs={{0,8},{1,9},{2,10},{3,11},{4,12},{5,13},{6,14},{7,15},{8,0},{9,1},... | collective-permute-start | bytes 589832 | tf_op jit(solution)/shard_map/ppermute | solution.py:21
  25.3 1.6 %copy-start.4 = (s32[4,32,32,128]{3,2,1,0:T(8,128)S(1)}, s32[4,32,32,128]{3,2,1,0:T(8,128)}, u32[]{:S(2)}) copy-start(s32[4,32,32,128]{3,2,1,0:T(8,128)} %flag_hbm.1) | copy-start | bytes 6291460
  26.9 37.0 %copy-start.6 = (f32[40,2048]{1,0:T(8,128)S(1)}, f32[40,2048]{1,0:T(8,128)}, u32[]{:S(2)}) copy-start(f32[40,2048]{1,0:T(8,128)} %shapes_ref.3) | copy-start | bytes 983044
  26.9 37.0 %copy-start.8 = (s32[4,32,32]{2,1,0:T(8,128)S(1)}, s32[4,32,32]{2,1,0:T(8,128)}, u32[]{:S(2)}) copy-start(s32[4,32,32]{2,1,0:T(8,128)} %param.13) | copy-start | bytes 49156
  26.9 37.0 %copy-start.9 = (f32[40]{0:T(128)S(1)}, f32[40]{0:T(128)}, u32[]{:S(2)}) copy-start(f32[40]{0:T(128)} %param.15) | copy-start | bytes 484

commit v2 on v1

--- a/solution.py
+++ b/solution.py
@@ -3,6 +3,7 @@
 
 import jax
 import jax.numpy as jnp
+import numpy as np
 from jax import lax
 from jax.experimental import pallas as pl
 from jax.experimental.pallas import tpu as pltpu
@@ -14,7 +15,7 @@
 DECK_GAIN = 0.15
 EPSILON = 1e-06
 LANES = 128
-VMEM_LIMIT = 40 * 1024 * 1024
+MIB = 1024 * 1024
 
 
 def swapped(x, axis, stride):
@@ -43,7 +44,7 @@
     found = []
     for face in range(4 * blocks):
         b, t = face // 4, face % 4
-        partner = links[b, t, 0]
+        partner = links[0, b, t]
         differ = (partner >> shift) ^ me
         k = jnp.int32(0)
         for q in range(1, bits):
@@ -51,25 +52,31 @@
         r = count[k]
         count[k] = r + 1
         sent[k * CAP + r] = face
-        source = (partner & (blocks - 1)) * 4 + links[b, t, 1]
+        source = (partner & (blocks - 1)) * 4 + links[1, b, t]
         mask[k] = mask[k] | (jnp.int32(1) << source)
         found.append((k, source))
     for face, (k, source) in enumerate(found):
         rank = set_bits(mask[k] & ((jnp.int32(1) << source) - 1))
-        got[k * CAP + rank] = 2 * face + links[face // 4, face % 4, 2]
-
-
-def pack_kernel(dims, links, node_ref, shapes_ref, fill_hbm, vel_hbm, *rest):
+        got[k * CAP + rank] = 2 * face + links[2, face // 4, face % 4]
+
+
+def pack_kernel(dims, links, node_hbm, shapes_hbm, fill_hbm, vel_hbm, *rest):
     blocks, ext, height, bits = dims
     outs = rest[:bits]
-    red_ref, got, fill, vel, edge, left, right, count, mask, sent, sems = rest[bits:]
+    red_ref, got, fill, vel, edge, left, right, node_ref, shapes_ref, count, mask, sent, sems, late = rest[bits:]
     area = ext * ext
     fill_copies, vel_copies = [], []
     for b in range(blocks):
         fill_copies.append(pltpu.make_async_copy(fill_hbm.at[b], fill.at[b], sems.at[0, b]))
         vel_copies.append(pltpu.make_async_copy(vel_hbm.at[b], vel.at[b], sems.at[1, b]))
+        vel_copies[b].start()
         fill_copies[b].start()
-        vel_copies[b].start()
+    late_copies = [
+        pltpu.make_async_copy(node_hbm, node_ref, late.at[0]),
+        pltpu.make_async_copy(shapes_hbm, shapes_ref, late.at[1]),
+    ]
+    for c in late_copies:
+        c.start()
     route(links, lax.axis_index("family"), blocks, bits, count, mask, sent, got)
     lane = lax.broadcasted_iota(jnp.int32, (ext, height), 1)
     rows = fill.reshape(blocks * area, height)
@@ -94,7 +101,7 @@
             pressure = jnp.where(lane == at, pltpu.roll(push, at + 1, 1), pressure)
             return pressure, speed
 
-        pressure, speed = lax.fori_loop(0, ext, step, (pressure, speed), unroll=4)
+        pressure, speed = lax.fori_loop(0, ext, step, (pressure, speed), unroll=True)
     for k in range(bits):
         for s in range(CAP):
             face = sent[k * CAP + s]
@@ -116,6 +123,8 @@
                 outs[k][s, 1] = rows[pl.ds(b * area + after, ext, stride=ext), :]
                 outs[k][s, 2] = edge[pl.ds((b * 2 + side) * ext * 8 + side * 7, ext, stride=8), :] * sign
 
+    for c in late_copies:
+        c.wait()
     node = node_ref[...].T
     high, low = node >> 7, node & 127
     groups = shapes_ref.shape[1] // LANES
@@ -144,58 +153,78 @@
     red_ref[...] = red
 
 
-def rates_kernel(dims, fill_hbm, start_hbm, vel_hbm, flag_hbm, base_ref, rate_ref, rim_ref, fill, start, vel, flag, edge, sems):
+def shift_tables(height):
+    k = np.arange(height)
+    eye = np.eye(height, dtype=np.float32)
+    nxt = np.eye(height, k=-1, dtype=np.float32)
+    nxt2 = np.eye(height, k=-2, dtype=np.float32)
+    prv = np.eye(height, k=1, dtype=np.float32)
+    before = 0.5 * (eye - prv); before[:, 0] = 0
+    step = 0.5 * (nxt - eye); step[:, -1] = 0
+    after = 0.5 * (nxt2 - nxt); after[:, -2:] = 0
+    cells = np.concatenate([before, step, after, nxt], 1)
+    flow = nxt + eye; flow[:, -1] = 0
+    return np.concatenate([cells, cells], 0), flow
+def rates_kernel(dims, cells_ref, flow_ref, fill, vel, start, flag, base_ref, rate_ref, rim_ref, top_ref, edge, lift):
     blocks, ext, height, bits = dims
     area = ext * ext
-    copies = []
-    for b in range(blocks):
-        group = [
-            pltpu.make_async_copy(fill_hbm.at[b], fill.at[b], sems.at[0, b]),
-            pltpu.make_async_copy(vel_hbm.at[b], vel.at[b], sems.at[1, b]),
-            pltpu.make_async_copy(flag_hbm.at[b], flag.at[b], sems.at[2, b]),
-            pltpu.make_async_copy(start_hbm.at[b], start.at[b], sems.at[3, b]),
-        ]
-        for c in group:
-            c.start()
-        copies.append(group)
     lane = lax.broadcasted_iota(jnp.int32, (ext, height), 1)
     row = lax.broadcasted_iota(jnp.int32, (ext, height), 0)
-    last_lane = lane == height - 1
     open_row = (row >= 1) & (row <= ext - 3)
     rows = fill.reshape(blocks * area, height)
-
-    def across(f, h, u, axis, size, cut, masked):
-        step = jnp.where(cut, 0.0, pltpu.roll(h, size - 1, axis) - h) if masked else pltpu.roll(h, size - 1, axis) - h
-        slope = limited(pltpu.roll(step, 1, axis), step)
-        behind = f - slope
-        v = u + pltpu.roll(u, size - 1, axis)
-        v = jnp.where(cut, 0.0, v)
-        flux = v * jnp.where(v > 0.0, f + slope, pltpu.roll(behind, size - 1, axis))
-        return pltpu.roll(flux, 1, axis) - flux
-
-    def own(b, i, f, h):
-        rate = across(f, h, vel[b, 2, i].astype(jnp.float32), 1, height, last_lane, True)
-        rate = rate + across(f, h, vel[b, 1, i].astype(jnp.float32), 0, ext, ~open_row, False)
-        sharp = (2.0 * SHARPEN) * f * (1.0 - f) * (2.0 * f - 1.0)
-        rate = rate + jnp.where(flag[b, i] != 0, sharp, 0.0)
-        base_ref[b, i] = 0.75 * start[b, i] + 0.25 * f
-        return rate
-
-    for b in range(blocks):
-        for c in copies[b]:
-            c.wait()
+    layers = 8
+    size = layers * ext
+    top = jnp.zeros((ext, height), jnp.float32)
+    def block(b, top):
+
+        def column(c, carry):
+            x = fill[b, pl.ds(c * layers, layers)].reshape(size, height)
+            u = vel[b, 2, pl.ds(c * layers, layers)].reshape(size, height)
+            high = x.astype(jnp.bfloat16)
+            low = (x - high.astype(jnp.float32)).astype(jnp.bfloat16)
+            y = jnp.dot(jnp.concatenate([high, low], 1), cells_ref[...], preferred_element_type=jnp.float32)
+            v = jnp.dot(u, flow_ref[...], preferred_element_type=jnp.float32)
+            step = y[:, height : 2 * height]
+            ahead = x + limited(step, y[:, :height])
+            behind = y[:, 3 * height :] - limited(step, y[:, 2 * height : 3 * height])
+            lift[pl.ds(c * layers, layers)] = (v * jnp.where(v > 0.0, ahead, behind)).reshape(layers, ext, height)
+            return carry
+
+        lax.fori_loop(0, ext // layers, column, 0, unroll=True)
+
+        def own(i, f, h):
+            flux = lift[i]
+            rate = pltpu.roll(flux, 1, 1) - flux
+            step = pltpu.roll(h, ext - 1, 0) - h
+            slope = limited(pltpu.roll(step, 1, 0), step)
+            u = vel[b, 1, i].astype(jnp.float32)
+            v = u + pltpu.roll(u, ext - 1, 0)
+            v = jnp.where(open_row, v, 0.0)
+            flux = v * jnp.where(v > 0.0, f + slope, pltpu.roll(f - slope, ext - 1, 0))
+            rate = rate + (pltpu.roll(flux, 1, 0) - flux)
+            sharp = (f * (1.0 - f)) * ((4.0 * SHARPEN) * f - 2.0 * SHARPEN)
+            rate = rate + jnp.where(flag[b, i] != 0, sharp, 0.0)
+            base_ref[b, i] = 0.75 * start[b, i] + 0.25 * f
+            return rate
+
+        def picked(i, f, top):
+            at = b * ext + i
+            return jnp.where(lane == at, pltpu.roll(f, at + 1, 1), top)
+
         f0 = fill[b, 0]
-        rate_ref[b, 0] = own(b, 0, f0, 0.5 * f0)
+        rate_ref[b, 0] = own(0, f0, 0.5 * f0)
+        top = picked(0, f0, top)
         f1 = fill[b, 1]
         h1 = 0.5 * f1
-        rate1 = own(b, 1, f1, h1)
+        rate1 = own(1, f1, h1)
+        top = picked(1, f1, top)
         f2 = fill[b, 2]
         h2 = 0.5 * f2
         step = h2 - h1
         ahead = f1 + limited(h1 - 0.5 * f0, step)
 
         def layer(i, carry):
-            f, h, step_before, ahead, flux_before, u_before, rate_before = carry
+            f, h, step_before, ahead, flux_before, u_before, rate_before, top = carry
             f_next = fill[b, i + 1]
             h_next = 0.5 * f_next
             step = h_next - h
@@ -204,13 +233,14 @@
             v = u_before + u
             flux = v * jnp.where(v > 0.0, ahead, f - slope)
             rate_ref[b, i - 1] = rate_before + (flux_before - flux)
-            return f_next, h_next, step, f + slope, flux, u, own(b, i, f, h)
-
-        carry = (f2, h2, step, ahead, jnp.zeros_like(f0), vel[b, 0, 1].astype(jnp.float32), rate1)
-        carry = lax.fori_loop(2, ext - 1, layer, carry)
-        f, h, _, _, flux, _, rate = carry
+            return f_next, h_next, step, f + slope, flux, u, own(i, f, h), picked(i, f, top)
+
+        carry = (f2, h2, step, ahead, jnp.zeros_like(f0), vel[b, 0, 1].astype(jnp.float32), rate1, top)
+        carry = lax.fori_loop(2, ext - 1, layer, carry, unroll=True)
+        f, h, _, _, flux, _, rate, top = carry
         rate_ref[b, ext - 2] = rate + flux
-        rate_ref[b, ext - 1] = own(b, ext - 1, f, h)
+        rate_ref[b, ext - 1] = own(ext - 1, f, h)
+        top = picked(ext - 1, f, top)
 
         for side in range(2):
             x = vel[b, 1, :, side * (ext - 8) : side * (ext - 8) + 8, :].astype(jnp.float32)
@@ -232,18 +262,17 @@
             rim_ref[4 * b + t, 2] = cells[1] - slope
             rim_ref[4 * b + t, 3] = flows[0]
             rim_ref[4 * b + t, 4] = flows[0] + flows[1]
-
-
-def final_kernel(dims, devices, got, mobility_ref, node_ref, shapes_ref, red_ref, base_ref, rate_ref, rim_ref, fill_hbm, *rest):
+        return top
+    top_ref[...] = lax.fori_loop(0, blocks, block, top)
+
+
+def final_kernel(dims, devices, got, mobility_ref, node_ref, shapes_ref, red_ref, base_ref, rate_ref, rim_ref, top_ref, *rest):
     blocks, ext, height, bits = dims
     ghosts = rest[:bits]
-    out_hbm, deck_ref, ghost, out, top_fill, sems, fsems = rest[bits:]
+    out_hbm, deck_ref, ghost, out, sems = rest[bits:]
     area = ext * ext
     tiles = shapes_ref.shape[0] // 8
     groups = shapes_ref.shape[1] // LANES
-    fill_copies = [pltpu.make_async_copy(fill_hbm.at[b], top_fill.at[b], fsems.at[b]) for b in range(blocks)]
-    for c in fill_copies:
-        c.start()
     turned = 7 - lax.broadcasted_iota(jnp.int32, (8, height), 0)
     for k in range(bits):
         for s in range(CAP):
@@ -288,8 +317,7 @@
     lane = lax.broadcasted_iota(jnp.int32, (ext, height), 1)
     last_lane = lane == height - 1
     rows = out.reshape(blocks * area, height)
-    twice = 2.0 * eighth
-    deck = deck * twice
+    deck = deck * (2.0 * eighth) * top_ref[...]
 
     def apply(ghost_face, rim_face):
         g0, g1, gv = ghost[ghost_face, 0], ghost[ghost_face, 1], ghost[ghost_face, 2]
@@ -304,15 +332,14 @@
 
     copies = []
     for b in range(blocks):
-        fill_copies[b].wait()
 
         def layer(i, carry):
             at = b * ext + i
             lid = jnp.where(last_lane, pltpu.roll(deck, height - 1 - at, 1), 0.0)
-            out[b, i] = base_ref[b, i] + eighth * rate_ref[b, i] - lid * top_fill[b, i]
+            out[b, i] = base_ref[b, i] + eighth * rate_ref[b, i] - lid
             return carry
 
-        lax.fori_loop(0, ext, layer, 0, unroll=4)
+        lax.fori_loop(0, ext, layer, 0, unroll=True)
         for t in range(4):
             side = t % 2
             near = side * (ext - 1)
@@ -331,6 +358,10 @@
         copy.wait()
 
 
+def in_hbm(x):
+    return pltpu.with_memory_space_constraint(x, pltpu.HBM)
+
+
 def local(fraction, fraction_start, velocity, interface_flags, block_links, deck_node, mode_shapes, mobility):
     blocks, ext, _, height = fraction.shape
     devices = lax.axis_size("family")
@@ -341,30 +372,36 @@
     f32 = jnp.float32
     vmem = pl.BlockSpec(memory_space=pltpu.VMEM)
     smem = pl.BlockSpec(memory_space=pltpu.SMEM)
-    hbm = pl.BlockSpec(memory_space=pl.ANY)
-    params = pltpu.CompilerParams(vmem_limit_bytes=VMEM_LIMIT)
+    hbm = pl.BlockSpec(memory_space=pltpu.HBM)
+    params = pltpu.CompilerParams(vmem_limit_bytes=24 * MIB)
     flat_node = deck_node.reshape(blocks * ext, ext)
     packed = pl.pallas_call(
         functools.partial(pack_kernel, dims),
-        out_shape=[jax.ShapeDtypeStruct((CAP, 3, ext, height), f32)] * bits
-        + [jax.ShapeDtypeStruct((8, LANES), f32), jax.ShapeDtypeStruct((bits * CAP,), jnp.int32)],
-        in_specs=[smem, vmem, vmem, hbm, hbm],
-        out_specs=[vmem] * (bits + 1) + [smem],
+        out_shape=[pltpu.VMEM((CAP, 3, ext, height), f32)] * bits
+        + [
+            pltpu.VMEM((8, LANES), f32),
+            pltpu.SMEM((bits * CAP,), jnp.int32),
+            pltpu.VMEM(fraction.shape, f32),
+            pltpu.VMEM(velocity.shape, jnp.bfloat16),
+        ],
+        in_specs=[smem, hbm, hbm, hbm, hbm],
+        out_specs=[vmem] * (bits + 1) + [smem, vmem, vmem],
         scratch_shapes=[
-            pltpu.VMEM((blocks, ext, ext, height), f32),
-            pltpu.VMEM((blocks, 3, ext, ext, height), jnp.bfloat16),
             pltpu.VMEM((blocks * 2 * ext * 8, height), f32),
             pltpu.VMEM((2 * nodes // LANES, ext * height), jnp.bfloat16),
             pltpu.VMEM((LANES, ext * height), jnp.bfloat16),
+            pltpu.VMEM((blocks * ext, ext), jnp.int32),
+            pltpu.VMEM((modes, nodes), f32),
             pltpu.SMEM((bits,), jnp.int32),
             pltpu.SMEM((bits,), jnp.int32),
             pltpu.SMEM((bits * CAP,), jnp.int32),
             pltpu.SemaphoreType.DMA((2, blocks)),
+            pltpu.SemaphoreType.DMA((2,)),
         ],
         compiler_params=params,
         name="pack",
-    )(block_links, flat_node, mode_shapes, fraction, velocity)
-    outgoing, red, got = packed[:bits], packed[bits], packed[bits + 1]
+    )(*(in_hbm(x) for x in (jnp.transpose(block_links, (2, 0, 1)), flat_node, mode_shapes, fraction, velocity)))
+    outgoing, (red, got, fill, vel) = packed[:bits], packed[bits:]
     received = [None] * bits
     for k in reversed(range(bits)):
         received[k] = swapped(outgoing[k], "family", k)
@@ -372,45 +409,41 @@
     for k in range(bits):
         other = swapped(red, "family", k)
         red = jnp.where(is_top, jnp.maximum(red, other), red + other)
-    base, rate, rim = pl.pallas_call(
+    cells, flow = shift_tables(height)
+    base, rate, rim, top = pl.pallas_call(
         functools.partial(rates_kernel, dims),
         out_shape=[
             jax.ShapeDtypeStruct(fraction.shape, f32),
             jax.ShapeDtypeStruct(fraction.shape, f32),
             jax.ShapeDtypeStruct((faces, 5, ext, height), f32),
-        ],
-        in_specs=[hbm] * 4,
-        out_specs=[vmem] * 3,
+            jax.ShapeDtypeStruct((ext, height), f32),
+        ],
+        in_specs=[vmem] * 6,
+        out_specs=[vmem] * 4,
         scratch_shapes=[
-            pltpu.VMEM((blocks, ext, ext, height), f32),
-            pltpu.VMEM((blocks, ext, ext, height), f32),
-            pltpu.VMEM((blocks, 3, ext, ext, height), jnp.bfloat16),
-            pltpu.VMEM((blocks, ext, ext, height), jnp.int32),
             pltpu.VMEM((2 * ext * 8, height), f32),
-            pltpu.SemaphoreType.DMA((4, blocks)),
+            pltpu.VMEM((ext, ext, height), f32),
         ],
         compiler_params=params,
         cost_estimate=pl.CostEstimate(flops=80 * fraction.size, bytes_accessed=20 * fraction.size, transcendentals=0),
         name="rates",
-    )(fraction, fraction_start, velocity, interface_flags)
+    )(jnp.asarray(cells, jnp.bfloat16), jnp.asarray(flow, jnp.bfloat16), fill, vel, fraction_start, interface_flags)
     updated, deck = pl.pallas_call(
         functools.partial(final_kernel, dims, devices),
         out_shape=[
             jax.ShapeDtypeStruct(fraction.shape, f32),
             jax.ShapeDtypeStruct((blocks * ext, ext), f32),
         ],
-        in_specs=[smem] + [vmem] * 7 + [hbm] + [vmem] * bits,
+        in_specs=[smem] + [vmem] * (8 + bits),
         out_specs=[hbm, vmem],
         scratch_shapes=[
             pltpu.VMEM((faces, 3, ext, height), f32),
             pltpu.VMEM((blocks, ext, ext, height), f32),
-            pltpu.VMEM((blocks, ext, ext, height), f32),
-            pltpu.SemaphoreType.DMA((blocks,)),
             pltpu.SemaphoreType.DMA((blocks,)),
         ],
         compiler_params=params,
         name="finish",
-    )(got, mobility.reshape(1, modes), flat_node, mode_shapes, red, base, rate, rim, fraction, *received)
+    )(got, mobility.reshape(1, modes), flat_node, mode_shapes, red, base, rate, rim, top, *received)
     return updated, deck.reshape(blocks, ext, ext)
 
 

time: 70.7 us -> 30.4 us (0.43)
  Pallas kernels: 49.2 us -> 14.8 us
  local copies, waits for them, and re-layouts: 7.7 us -> 0.04 us
  waiting for transfers between devices: 2.42 us -> 4.23 us
    pallas_call x1, Pallas kernels: 36.9 us -> 6.04 us  [local(): pl.pallas_call(functools.partial(rates_kernel, dims), out_shape=[jax.Shap...]
    unnamed x21 -> x14, local copies, waits for them, and re-layouts: 7.7 us -> 0.04 us
    pallas_call x1, Pallas kernels: 6.48 us -> 3.23 us  [local(): pl.pallas_call(functools.partial(final_kernel, dims, devices), out_shape=...]
    ppermute x8, waiting for transfers between devices: 2.42 us -> 4.23 us  [swapped(): lax.ppermute(x, axis, [(i, i ^ 1 << stride) for i in range(lax.axis_size(...]
  transfers between devices with their start and end apart: 8 -> 8, of which waited for: 2 -> 3; matrix products, arithmetic and copies ran while one was open for 0% -> 0% of each run, Pallas kernels for 52% -> 20%
where the time goes in v2:
time: 30.4 us; the launch traced here: 30.2 us
  Pallas kernels  14.8 us (49%)
  starting transfers between devices  10.4 us (34%)
  waiting for transfers between devices  4.23 us (14%)
  between operations  0.76 us (2%)
    ppermute x8, starting transfers between devices, swapped(): lax.ppermute(x, axis, [(i, i ^ 1 << stride) for i in range(lax.axis_size(...  10.4 us
    pallas_call x1, Pallas kernels, local(): pl.pallas_call(functools.partial(rates_kernel, dims), out_shape=[jax.Shap...  6.04 us
    pallas_call x1, Pallas kernels, local(): pl.pallas_call(functools.partial(pack_kernel, dims), out_shape=[pltpu.VME...  5.5 us
    ppermute x8, waiting for transfers between devices, swapped(): lax.ppermute(x, axis, [(i, i ^ 1 << stride) for i in range(lax.axis_size(...  4.23 us
    pallas_call x1, Pallas kernels, local(): pl.pallas_call(functools.partial(final_kernel, dims, devices), out_shape=...  3.23 us
  transfers between devices with their start and end apart: 8, of which 3 were waited for; matrix products, arithmetic and copies ran while one was open for 0% of the time, Pallas kernels for 20%

profile of v2, /device:TPU:0, one launch (start us, length us, event | category | flops | bytes accessed | tf_op | source)
XLA Modules:
  0.0 30.2 jit_solution(9733113960859134021)
XLA Ops:
  0.6 0.0 copy-start
  0.6 0.0 copy-start.1
  0.7 0.0 copy-start.4
  0.7 0.0 copy-start.5
  0.7 5.5 %pack.1 = (f32[4,3,32,128]{3,2,1,0:T(8,128)S(1)}, f32[4,3,32,128]{3,2,1,0:T(8,128)S(1)}, f32[4,3,32,128]{3,2,1,0:T(8,128)S(1)}, f32[4,3,32,128]{3,2,1,0:T(8,128)...) custom-call(s32[3,4,4]{2,1,0:T(4,128)} %bitcast.7, ...), custom_call_target="tpu_custom_call" | custom-call | tf_op jit(solution)/shard_map/pack/pallas_call | solution.py:378
  6.2 0.5 %collective-permute-start = (f32[8,128]{1,0:T(8,128)S(1)}, f32[8,128]{1,0:T(8,128)S(1)}, u32[]{:S(2)}, u32[]{:S(2)}) collective-permute-start(f32[8,128]{1,0:T(8,128)S(1)} %get-tuple-element.17), channel_id=1, source_target_pairs={{0,1},{1,0},{2,3},{3,2},{4,5},{5,4},{6,7},{7,6},{8,9},{9,8},{10,11... | collective-permute-start | bytes 12296 | tf_op jit(solution)/shard_map/ppermute | solution.py:22
  6.7 0.8 %collective-permute-done = f32[8,128]{1,0:T(8,128)S(1)} collective-permute-done((f32[8,128]{1,0:T(8,128)S(1)}, f32[8,128]{1,0:T(8,128)S(1)}, u32[]{:S(2)}, u32[]{:S(2)}) %collective-permute-start) | collective-permute-done | bytes 4128 | tf_op jit(solution)/shard_map/ppermute | solution.py:22
  7.5 2.9 %collective-permute-start.1 = (f32[8,128]{1,0:T(8,128)S(1)}, f32[8,128]{1,0:T(8,128)S(1)}, u32[]{:S(2)}, u32[]{:S(2)}) collective-permute-start(f32[8,128]{1,0:T(8,128)S(1)} %add_select_fusion.3), channel_id=1, source_target_pairs={{0,2},{1,3},{2,0},{3,1},{4,6},{5,7},{6,4},{7,5},{8,10},{9,11},{10,... | collective-permute-start | bytes 12296 | tf_op jit(solution)/shard_map/ppermute | solution.py:22
  10.4 1.6 %collective-permute-done.1 = f32[8,128]{1,0:T(8,128)S(1)} collective-permute-done((f32[8,128]{1,0:T(8,128)S(1)}, f32[8,128]{1,0:T(8,128)S(1)}, u32[]{:S(2)}, u32[]{:S(2)}) %collective-permute-start.1) | collective-permute-done | bytes 4128 | tf_op jit(solution)/shard_map/ppermute | solution.py:22
  12.0 2.1 %collective-permute-start.2 = (f32[8,128]{1,0:T(8,128)S(1)}, f32[8,128]{1,0:T(8,128)S(1)}, u32[]{:S(2)}, u32[]{:S(2)}) collective-permute-start(f32[8,128]{1,0:T(8,128)S(1)} %add_select_fusion.2), channel_id=1, source_target_pairs={{0,4},{1,5},{2,6},{3,7},{4,0},{5,1},{6,2},{7,3},{8,12},{9,13},{10,... | collective-permute-start | bytes 12296 | tf_op jit(solution)/shard_map/ppermute | solution.py:22
  14.1 0.0 collective-permute-start.4
  14.1 1.5 %collective-permute-start.5 = (f32[4,3,32,128]{3,2,1,0:T(8,128)S(1)}, f32[4,3,32,128]{3,2,1,0:T(8,128)S(1)}, u32[]{:S(2)}, u32[]{:S(2)}) collective-permute-start(f32[4,3,32,128]{3,2,1,0:T(8,128)S(1)} %get-tuple-element.25), channel_id=1, source_target_pairs={{0,2},{1,3},{2,0},{3,1},{4,6},{5,7},{6,4},{7,5},{8,10},{9,11},{10,... | collective-permute-start | bytes 589832 | tf_op jit(solution)/shard_map/ppermute | solution.py:22
  15.6 0.4 %collective-permute-start.6 = (f32[4,3,32,128]{3,2,1,0:T(8,128)S(1)}, f32[4,3,32,128]{3,2,1,0:T(8,128)S(1)}, u32[]{:S(2)}, u32[]{:S(2)}) collective-permute-start(f32[4,3,32,128]{3,2,1,0:T(8,128)S(1)} %get-tuple-element.26), channel_id=1, source_target_pairs={{0,4},{1,5},{2,6},{3,7},{4,0},{5,1},{6,2},{7,3},{8,12},{9,13},{10,... | collective-permute-start | bytes 589832 | tf_op jit(solution)/shard_map/ppermute | solution.py:22
  16.0 2.6 %collective-permute-start.7 = (f32[4,3,32,128]{3,2,1,0:T(8,128)S(1)}, f32[4,3,32,128]{3,2,1,0:T(8,128)S(1)}, u32[]{:S(2)}, u32[]{:S(2)}) collective-permute-start(f32[4,3,32,128]{3,2,1,0:T(8,128)S(1)} %get-tuple-element.27), channel_id=1, source_target_pairs={{0,8},{1,9},{2,10},{3,11},{4,12},{5,13},{6,14},{7,15},{8,0},{9,1},... | collective-permute-start | bytes 589832 | tf_op jit(solution)/shard_map/ppermute | solution.py:22
  18.6 0.0 collective-permute-done.2
  18.6 0.3 %collective-permute-start.3 = (f32[8,128]{1,0:T(8,128)S(1)}, f32[8,128]{1,0:T(8,128)S(1)}, u32[]{:S(2)}, u32[]{:S(2)}) collective-permute-start(f32[8,128]{1,0:T(8,128)S(1)} %add_select_fusion.1), channel_id=1, source_target_pairs={{0,8},{1,9},{2,10},{3,11},{4,12},{5,13},{6,14},{7,15},{8,0},{9,1},... | collective-permute-start | bytes 12296 | tf_op jit(solution)/shard_map/ppermute | solution.py:22
  19.0 0.0 copy-done
  19.0 0.0 copy-done.1
  19.0 0.0 copy-done.4
  19.0 0.0 copy-done.5
  19.0 0.0 copy-start.2
  19.0 0.0 copy-start.3
  19.0 0.0 copy-start.6
  19.0 6.0 %rates.1 = (f32[4,32,32,128]{3,2,1,0:T(8,128)S(1)}, f32[4,32,32,128]{3,2,1,0:T(8,128)S(1)}, f32[16,5,32,128]{3,2,1,0:T(8,128)S(1)}, f32[32,128]{1,0:T(8,128)S(1)}) custom-call(bf16[256,512]{1,0:T(8,128)(2,1)S(1)} %copy-done.4, bf16[128,128]{1,0:T(8,128)(2,1)S(1)} %copy-done.5, f32[4,32,32,128]{3,2,1,0:T(8,128)S(1)} %get-tuple-element.18.fill, ...), custom_call_target="tpu_custom_call" | custom-call | flops 41943040 | bytes 10485760 | tf_op jit(solution)/shard_map/rates/pallas_call | solution.py:413
  25.1 0.0 collective-permute-done.3
  25.1 0.0 collective-permute-done.4.rest_0_
  25.1 0.0 collective-permute-done.5.rest_1_
  25.1 1.8 %collective-permute-done.6.rest_2_ = f32[4,3,32,128]{3,2,1,0:T(8,128)S(1)} collective-permute-done((f32[4,3,32,128]{3,2,1,0:T(8,128)S(1)}, f32[4,3,32,128]{3,2,1,0:T(8,128)S(1)}, u32[]{:S(2)}, u32[]{:S(2)}) %collective-permute-start.6) | collective-permute-done | bytes 196640 | tf_op jit(solution)/shard_map/ppermute | solution.py:22
  26.9 0.0 collective-permute-done.7.rest_3_
  26.9 0.0 copy-done.2
  26.9 0.0 copy-done.3
  26.9 3.2 %finish.1 = (f32[4,32,32,128]{3,2,1,0:T(8,128)}, f32[128,32]{1,0:T(8,128)}) custom-call(s32[16]{0:T(128)S(4)} %get-tuple-element.16.got, f32[1,40]{1,0:T(1,128)S(1)} %bitcast.6, s32[128,32]{1,0:T(8,128)S(1)} %bitcast.5, f32[40,2048]{1,0:T(8,128)S(1)} %copy-done.2, f32[8,128]{1,0:T(8,128)S(1)} %add_select_fusion.red_ref, ...), custom_call_target="tpu_custom_call" | custom-call | tf_op jit(solution)/shard_map/finish/pallas_call | solution.py:431
  (6 shorter events, 0.0 us)
Async XLA Ops:
  0.6 18.3 %copy-start = (f32[4,32,32,128]{3,2,1,0:T(8,128)S(1)}, f32[4,32,32,128]{3,2,1,0:T(8,128)}, u32[]{:S(2)}) copy-start(f32[4,32,32,128]{3,2,1,0:T(8,128)} %start.1) | copy-start | bytes 6291460
  0.6 18.3 %copy-start.1 = (s32[4,32,32,128]{3,2,1,0:T(8,128)S(1)}, s32[4,32,32,128]{3,2,1,0:T(8,128)}, u32[]{:S(2)}) copy-start(s32[4,32,32,128]{3,2,1,0:T(8,128)} %flag.1) | copy-start | bytes 6291460
  0.7 18.3 %copy-start.4 = (bf16[256,512]{1,0:T(8,128)(2,1)S(1)}, bf16[256,512]{1,0:T(8,128)(2,1)}, u32[]{:S(2)}) copy-start(bf16[256,512]{1,0:T(8,128)(2,1)} %constant.6.clone.cells_ref) | copy-start | bytes 786436
  0.7 18.3 %copy-start.5 = (bf16[128,128]{1,0:T(8,128)(2,1)S(1)}, bf16[128,128]{1,0:T(8,128)(2,1)}, u32[]{:S(2)}) copy-start(bf16[128,128]{1,0:T(8,128)(2,1)} %constant.7.clone.flow_ref) | copy-start | bytes 98308
  6.2 1.3 %collective-permute-start = (f32[8,128]{1,0:T(8,128)S(1)}, f32[8,128]{1,0:T(8,128)S(1)}, u32[]{:S(2)}, u32[]{:S(2)}) collective-permute-start(f32[8,128]{1,0:T(8,128)S(1)} %get-tuple-element.17), channel_id=1, source_target_pairs={{0,1},{1,0},{2,3},{3,2},{4,5},{5,4},{6,7},{7,6},{8,9},{9,8},{10,11... | collective-permute-start | bytes 12296 | tf_op jit(solution)/shard_map/ppermute | solution.py:22
  7.5 4.4 %collective-permute-start.1 = (f32[8,128]{1,0:T(8,128)S(1)}, f32[8,128]{1,0:T(8,128)S(1)}, u32[]{:S(2)}, u32[]{:S(2)}) collective-permute-start(f32[8,128]{1,0:T(8,128)S(1)} %add_select_fusion.3), channel_id=1, source_target_pairs={{0,2},{1,3},{2,0},{3,1},{4,6},{5,7},{6,4},{7,5},{8,10},{9,11},{10,... | collective-permute-start | bytes 12296 | tf_op jit(solution)/shard_map/ppermute | solution.py:22
  12.0 6.6 %collective-permute-start.2 = (f32[8,128]{1,0:T(8,128)S(1)}, f32[8,128]{1,0:T(8,128)S(1)}, u32[]{:S(2)}, u32[]{:S(2)}) collective-permute-start(f32[8,128]{1,0:T(8,128)S(1)} %add_select_fusion.2), channel_id=1, source_target_pairs={{0,4},{1,5},{2,6},{3,7},{4,0},{5,1},{6,2},{7,3},{8,12},{9,13},{10,... | collective-permute-start | bytes 12296 | tf_op jit(solution)/shard_map/ppermute | solution.py:22
  14.1 11.0 %collective-permute-start.4 = (f32[4,3,32,128]{3,2,1,0:T(8,128)S(1)}, f32[4,3,32,128]{3,2,1,0:T(8,128)S(1)}, u32[]{:S(2)}, u32[]{:S(2)}) collective-permute-start(f32[4,3,32,128]{3,2,1,0:T(8,128)S(1)} %get-tuple-element.24), channel_id=1, source_target_pairs={{0,1},{1,0},{2,3},{3,2},{4,5},{5,4},{6,7},{7,6},{8,9},{9,8},{10,11... | collective-permute-start | bytes 589832 | tf_op jit(solution)/shard_map/ppermute | solution.py:22
  14.1 11.0 %collective-permute-start.5 = (f32[4,3,32,128]{3,2,1,0:T(8,128)S(1)}, f32[4,3,32,128]{3,2,1,0:T(8,128)S(1)}, u32[]{:S(2)}, u32[]{:S(2)}) collective-permute-start(f32[4,3,32,128]{3,2,1,0:T(8,128)S(1)} %get-tuple-element.25), channel_id=1, source_target_pairs={{0,2},{1,3},{2,0},{3,1},{4,6},{5,7},{6,4},{7,5},{8,10},{9,11},{10,... | collective-permute-start | bytes 589832 | tf_op jit(solution)/shard_map/ppermute | solution.py:22
  15.6 11.3 %collective-permute-start.6 = (f32[4,3,32,128]{3,2,1,0:T(8,128)S(1)}, f32[4,3,32,128]{3,2,1,0:T(8,128)S(1)}, u32[]{:S(2)}, u32[]{:S(2)}) collective-permute-start(f32[4,3,32,128]{3,2,1,0:T(8,128)S(1)} %get-tuple-element.26), channel_id=1, source_target_pairs={{0,4},{1,5},{2,6},{3,7},{4,0},{5,1},{6,2},{7,3},{8,12},{9,13},{10,... | collective-permute-start | bytes 589832 | tf_op jit(solution)/shard_map/ppermute | solution.py:22
  16.0 10.9 %collective-permute-start.7 = (f32[4,3,32,128]{3,2,1,0:T(8,128)S(1)}, f32[4,3,32,128]{3,2,1,0:T(8,128)S(1)}, u32[]{:S(2)}, u32[]{:S(2)}) collective-permute-start(f32[4,3,32,128]{3,2,1,0:T(8,128)S(1)} %get-tuple-element.27), channel_id=1, source_target_pairs={{0,8},{1,9},{2,10},{3,11},{4,12},{5,13},{6,14},{7,15},{8,0},{9,1},... | collective-permute-start | bytes 589832 | tf_op jit(solution)/shard_map/ppermute | solution.py:22
  18.6 6.4 %collective-permute-start.3 = (f32[8,128]{1,0:T(8,128)S(1)}, f32[8,128]{1,0:T(8,128)S(1)}, u32[]{:S(2)}, u32[]{:S(2)}) collective-permute-start(f32[8,128]{1,0:T(8,128)S(1)} %add_select_fusion.1), channel_id=1, source_target_pairs={{0,8},{1,9},{2,10},{3,11},{4,12},{5,13},{6,14},{7,15},{8,0},{9,1},... | collective-permute-start | bytes 12296 | tf_op jit(solution)/shard_map/ppermute | solution.py:22
  19.0 7.9 %copy-start.2 = (f32[40,2048]{1,0:T(8,128)S(1)}, f32[40,2048]{1,0:T(8,128)}, u32[]{:S(2)}) copy-start(f32[40,2048]{1,0:T(8,128)} %shapes_ref.1) | copy-start | bytes 983044
  19.0 7.9 %copy-start.3 = (s32[4,32,32]{2,1,0:T(8,128)S(1)}, s32[4,32,32]{2,1,0:T(8,128)}, u32[]{:S(2)}) copy-start(s32[4,32,32]{2,1,0:T(8,128)} %param.15) | copy-start | bytes 49156
  19.0 7.9 %copy-start.6 = (f32[40]{0:T(128)S(1)}, f32[40]{0:T(128)}, u32[]{:S(2)}) copy-start(f32[40]{0:T(128)} %param.17) | copy-start | bytes 484

commit v3 on v2

--- a/solution.py
+++ b/solution.py
@@ -16,10 +16,11 @@
 EPSILON = 1e-06
 LANES = 128
 MIB = 1024 * 1024
-
-
-def swapped(x, axis, stride):
-    return lax.ppermute(x, axis, [(i, i ^ 1 << stride) for i in range(lax.axis_size(axis))])
+RATES_BYTES = 10 * MIB
+
+
+def crossed(x, axis, mask):
+    return lax.ppermute(x, axis, [(i, i ^ mask) for i in range(lax.axis_size(axis))])
 
 
 def limited(first, second):
@@ -60,34 +61,64 @@
         got[k * CAP + rank] = 2 * face + links[2, face // 4, face % 4]
 
 
-def pack_kernel(dims, links, node_hbm, shapes_hbm, fill_hbm, vel_hbm, *rest):
+def pack_kernel(dims, tiles, links, fill, vel, *rest):
     blocks, ext, height, bits = dims
     outs = rest[:bits]
-    red_ref, got, fill, vel, edge, left, right, node_ref, shapes_ref, count, mask, sent, sems, late = rest[bits:]
+    got, top_at, edge, count, mask, sent = rest[bits:]
+    top_at[...] = (lax.broadcasted_iota(jnp.int32, top_at.shape, 1) == tiles).astype(jnp.float32)
     area = ext * ext
+    route(links, lax.axis_index("family"), blocks, bits, count, mask, sent, got)
+    for b in range(blocks):
+        for side in range(2):
+            x = vel[b, 1, :, side * (ext - 16) : side * (ext - 16) + 16, :].astype(jnp.float32)[:, 8 * side : 8 * side + 8]
+            edge[pl.ds((b * 2 + side) * ext * 8, ext * 8), :] = x.reshape(ext * 8, height)
+    rows = fill.reshape(blocks * area, height)
+    for k in range(bits):
+        for s in range(CAP):
+            face = sent[k * CAP + s]
+            b, t = face >> 2, face & 3
+            side = t & 1
+            sign = (2 * side - 1).astype(jnp.float32)
+            near = side * (ext - 1)
+            after = near + 1 - 2 * side
+
+            @pl.when(t < 2)
+            def _():
+                outs[k][s, 0] = fill[b, near]
+                outs[k][s, 1] = fill[b, after]
+                outs[k][s, 2] = vel[b, 0, near].astype(jnp.float32) * sign
+
+            @pl.when(t >= 2)
+            def _():
+                outs[k][s, 0] = rows[pl.ds(b * area + near, ext, stride=ext), :]
+                outs[k][s, 1] = rows[pl.ds(b * area + after, ext, stride=ext), :]
+                outs[k][s, 2] = edge[pl.ds((b * 2 + side) * ext * 8 + side * 7, ext, stride=8), :] * sign
+
+
+def reduce_kernel(dims, node_hbm, shapes_hbm, fill_hbm, vel_hbm, red_ref, fill, vel, left, right, node_ref, shapes_ref, sems, late):
+    blocks, ext, height, bits = dims
+    early = pltpu.make_async_copy(node_hbm, node_ref, late.at[0])
+    early.start()
     fill_copies, vel_copies = [], []
     for b in range(blocks):
         fill_copies.append(pltpu.make_async_copy(fill_hbm.at[b], fill.at[b], sems.at[0, b]))
         vel_copies.append(pltpu.make_async_copy(vel_hbm.at[b], vel.at[b], sems.at[1, b]))
         vel_copies[b].start()
         fill_copies[b].start()
-    late_copies = [
-        pltpu.make_async_copy(node_hbm, node_ref, late.at[0]),
-        pltpu.make_async_copy(shapes_hbm, shapes_ref, late.at[1]),
-    ]
-    for c in late_copies:
-        c.start()
-    route(links, lax.axis_index("family"), blocks, bits, count, mask, sent, got)
+    last = pltpu.make_async_copy(shapes_hbm, shapes_ref, late.at[1])
+    last.start()
+    early.wait()
+    node = node_ref[...].T
+    high, low = node >> 7, node & 127
+    low_at = lax.broadcasted_iota(jnp.int32, (LANES, height), 0)
+    for j in range(ext):
+        right[:, j * height : (j + 1) * height] = jnp.where(low_at == low[j : j + 1], 1.0, 0.0).astype(jnp.bfloat16)
     lane = lax.broadcasted_iota(jnp.int32, (ext, height), 1)
-    rows = fill.reshape(blocks * area, height)
     pressure = jnp.zeros((ext, height), jnp.float32)
     speed = jnp.zeros((ext, height), jnp.bfloat16)
     for b in range(blocks):
+        vel_copies[b].wait()
         fill_copies[b].wait()
-        vel_copies[b].wait()
-        for side in range(2):
-            x = vel[b, 1, :, side * (ext - 8) : side * (ext - 8) + 8, :].astype(jnp.float32)
-            edge[pl.ds((b * 2 + side) * ext * 8, ext * 8), :] = x.reshape(ext * 8, height)
 
         def step(i, carry):
             pressure, speed = carry
@@ -102,43 +133,16 @@
             return pressure, speed
 
         pressure, speed = lax.fori_loop(0, ext, step, (pressure, speed), unroll=True)
-    for k in range(bits):
-        for s in range(CAP):
-            face = sent[k * CAP + s]
-            b, t = face >> 2, face & 3
-            side = t & 1
-            sign = (2 * side - 1).astype(jnp.float32)
-            near = side * (ext - 1)
-            after = near + 1 - 2 * side
-
-            @pl.when(t < 2)
-            def _():
-                outs[k][s, 0] = fill[b, near]
-                outs[k][s, 1] = fill[b, after]
-                outs[k][s, 2] = vel[b, 0, near].astype(jnp.float32) * sign
-
-            @pl.when(t >= 2)
-            def _():
-                outs[k][s, 0] = rows[pl.ds(b * area + near, ext, stride=ext), :]
-                outs[k][s, 1] = rows[pl.ds(b * area + after, ext, stride=ext), :]
-                outs[k][s, 2] = edge[pl.ds((b * 2 + side) * ext * 8 + side * 7, ext, stride=8), :] * sign
-
-    for c in late_copies:
-        c.wait()
-    node = node_ref[...].T
-    high, low = node >> 7, node & 127
+    last.wait()
     groups = shapes_ref.shape[1] // LANES
-    part = pressure.astype(jnp.bfloat16)
-    first = part.astype(jnp.float32)
+    first = pressure.astype(jnp.bfloat16).astype(jnp.float32)
     second = pressure - first
     high_at = lax.broadcasted_iota(jnp.int32, (groups, height), 0)
-    low_at = lax.broadcasted_iota(jnp.int32, (LANES, height), 0)
     for j in range(ext):
+        same = high_at == high[j : j + 1]
         cols = pl.ds(j * height, height)
-        same = high_at == high[j : j + 1]
         left[0:groups, cols] = jnp.where(same, first[j : j + 1], 0.0).astype(jnp.bfloat16)
         left[groups : 2 * groups, cols] = jnp.where(same, second[j : j + 1], 0.0).astype(jnp.bfloat16)
-        right[:, cols] = jnp.where(low_at == low[j : j + 1], 1.0, 0.0).astype(jnp.bfloat16)
     nodal = lax.dot_general(left[...], right[...], (((1,), (1,)), ((), ())), preferred_element_type=jnp.float32)
     nodal = nodal[:groups] + nodal[groups:]
     lane8 = lax.broadcasted_iota(jnp.int32, (8, LANES), 1)
@@ -243,7 +247,7 @@
         top = picked(ext - 1, f, top)
 
         for side in range(2):
-            x = vel[b, 1, :, side * (ext - 8) : side * (ext - 8) + 8, :].astype(jnp.float32)
+            x = vel[b, 1, :, side * (ext - 16) : side * (ext - 16) + 16, :].astype(jnp.float32)[:, 8 * side : 8 * side + 8]
             edge[pl.ds(side * ext * 8, ext * 8), :] = x.reshape(ext * 8, height)
         for t in range(4):
             side = t % 2
@@ -266,30 +270,11 @@
     top_ref[...] = lax.fori_loop(0, blocks, block, top)
 
 
-def final_kernel(dims, devices, got, mobility_ref, node_ref, shapes_ref, red_ref, base_ref, rate_ref, rim_ref, top_ref, *rest):
+def update_kernel(dims, devices, mobility_ref, node_ref, shapes_ref, red_ref, base_ref, rate_ref, top_ref, out, deck_ref, scale_ref):
     blocks, ext, height, bits = dims
-    ghosts = rest[:bits]
-    out_hbm, deck_ref, ghost, out, sems = rest[bits:]
     area = ext * ext
     tiles = shapes_ref.shape[0] // 8
     groups = shapes_ref.shape[1] // LANES
-    turned = 7 - lax.broadcasted_iota(jnp.int32, (8, height), 0)
-    for k in range(bits):
-        for s in range(CAP):
-            code = got[k * CAP + s]
-            face, flip = code >> 1, code & 1
-
-            @pl.when((code >= 0) & (flip == 0))
-            def _():
-                ghost[face] = ghosts[k][s]
-
-            @pl.when((code >= 0) & (flip == 1))
-            def _():
-                for c in range(3):
-                    for q in range(ext // 8):
-                        x = ghosts[k][s, c, ext - 8 - 8 * q : ext - 8 * q, :]
-                        ghost[face, c, 8 * q : 8 * q + 8, :] = jnp.take_along_axis(x, turned, axis=0)
-
     red = red_ref[...]
     time_step = CFL_NUMBER / (red[0:1, tiles : tiles + 1] + EPSILON)
     eighth = 0.125 * time_step
@@ -316,21 +301,9 @@
     deck_ref[...] = deck.T
     lane = lax.broadcasted_iota(jnp.int32, (ext, height), 1)
     last_lane = lane == height - 1
-    rows = out.reshape(blocks * area, height)
     deck = deck * (2.0 * eighth) * top_ref[...]
 
-    def apply(ghost_face, rim_face):
-        g0, g1, gv = ghost[ghost_face, 0], ghost[ghost_face, 1], ghost[ghost_face, 2]
-        c0, step1, behind1, u0, v1 = (rim_ref[rim_face, q] for q in range(5))
-        step0 = 0.5 * (c0 - g0)
-        ghost_slope = limited(step0, 0.5 * (g0 - g1))
-        slope = limited(step0, step1)
-        v0 = gv + u0
-        flux0 = v0 * jnp.where(v0 > 0.0, g0 + ghost_slope, c0 - slope)
-        flux1 = v1 * jnp.where(v1 > 0.0, c0 + slope, behind1)
-        return eighth * (flux0 - flux1), eighth * flux1
-
-    copies = []
+    scale_ref[...] = jnp.broadcast_to(eighth, scale_ref.shape)
     for b in range(blocks):
 
         def layer(i, carry):
@@ -340,18 +313,54 @@
             return carry
 
         lax.fori_loop(0, ext, layer, 0, unroll=True)
+
+
+def final_kernel(dims, got, scale_ref, rim_ref, part_in, *rest):
+    blocks, ext, height, bits = dims
+    ghosts = rest[:bits]
+    out_hbm, part, ghost, sems = rest[bits:]
+    area = ext * ext
+    turned = 7 - lax.broadcasted_iota(jnp.int32, (8, height), 0)
+    for k in range(bits):
+        for s in range(CAP):
+            code = got[k * CAP + s]
+            face, flip = code >> 1, code & 1
+
+            @pl.when((code >= 0) & (flip == 0))
+            def _():
+                ghost[face] = ghosts[k][s]
+
+            @pl.when((code >= 0) & (flip == 1))
+            def _():
+                for c in range(3):
+                    for q in range(ext // 8):
+                        x = ghosts[k][s, c, ext - 8 - 8 * q : ext - 8 * q, :]
+                        ghost[face, c, 8 * q : 8 * q + 8, :] = jnp.take_along_axis(x, turned, axis=0)
+
+    rows = part.reshape(blocks * area, height)
+    eighth = scale_ref[0:1, 0:1]
+    copies = []
+    for b in range(blocks):
         for t in range(4):
+            face = 4 * b + t
             side = t % 2
             near = side * (ext - 1)
             after = near + 1 - 2 * side
-            add0, add1 = apply(4 * b + t, 4 * b + t)
-            for where, add in ((near, add0), (after, add1)):
+            g0, g1, gv = ghost[face, 0], ghost[face, 1], ghost[face, 2]
+            c0, step1, behind1, u0, v1 = (rim_ref[face, q] for q in range(5))
+            step0 = 0.5 * (c0 - g0)
+            ghost_slope = limited(step0, 0.5 * (g0 - g1))
+            slope = limited(step0, step1)
+            v0 = gv + u0
+            flux0 = v0 * jnp.where(v0 > 0.0, g0 + ghost_slope, c0 - slope)
+            flux1 = v1 * jnp.where(v1 > 0.0, c0 + slope, behind1)
+            for where, add in ((near, eighth * (flux0 - flux1)), (after, eighth * flux1)):
                 if t < 2:
-                    out[b, where] = out[b, where] + add
+                    part[b, where] = part[b, where] + add
                 else:
                     line = pl.ds(b * area + where, ext, stride=ext)
                     rows[line, :] = rows[line, :] + add
-        copy = pltpu.make_async_copy(out.at[b], out_hbm.at[b], sems.at[b])
+        copy = pltpu.make_async_copy(part.at[b], out_hbm.at[b], sems.at[b])
         copy.start()
         copies.append(copy)
     for copy in copies:
@@ -375,41 +384,45 @@
     hbm = pl.BlockSpec(memory_space=pltpu.HBM)
     params = pltpu.CompilerParams(vmem_limit_bytes=24 * MIB)
     flat_node = deck_node.reshape(blocks * ext, ext)
-    packed = pl.pallas_call(
-        functools.partial(pack_kernel, dims),
-        out_shape=[pltpu.VMEM((CAP, 3, ext, height), f32)] * bits
-        + [
-            pltpu.VMEM((8, LANES), f32),
-            pltpu.SMEM((bits * CAP,), jnp.int32),
-            pltpu.VMEM(fraction.shape, f32),
-            pltpu.VMEM(velocity.shape, jnp.bfloat16),
-        ],
-        in_specs=[smem, hbm, hbm, hbm, hbm],
-        out_specs=[vmem] * (bits + 1) + [smem, vmem, vmem],
+    tables = [jnp.asarray(x, jnp.bfloat16) for x in shift_tables(height)]
+    red, fill, vel = pl.pallas_call(
+        functools.partial(reduce_kernel, dims),
+        out_shape=[pltpu.VMEM((8, LANES), f32), pltpu.VMEM(fraction.shape, f32), pltpu.VMEM(velocity.shape, jnp.bfloat16)],
+        in_specs=[hbm] * 4,
+        out_specs=[vmem] * 3,
         scratch_shapes=[
-            pltpu.VMEM((blocks * 2 * ext * 8, height), f32),
             pltpu.VMEM((2 * nodes // LANES, ext * height), jnp.bfloat16),
             pltpu.VMEM((LANES, ext * height), jnp.bfloat16),
             pltpu.VMEM((blocks * ext, ext), jnp.int32),
             pltpu.VMEM((modes, nodes), f32),
+            pltpu.SemaphoreType.DMA((2, blocks)),
+            pltpu.SemaphoreType.DMA((2,)),
+        ],
+        compiler_params=params,
+        name="reduce",
+    )(*(in_hbm(x) for x in (flat_node, mode_shapes, fraction, velocity)))
+    packed = pl.pallas_call(
+        functools.partial(pack_kernel, dims, modes // 8),
+        out_shape=[pltpu.VMEM((CAP, 3, ext, height), f32)] * bits + [pltpu.SMEM((bits * CAP,), jnp.int32), pltpu.VMEM((8, LANES), f32)],
+        in_specs=[smem, vmem, vmem],
+        out_specs=[vmem] * bits + [smem, vmem],
+        scratch_shapes=[
+            pltpu.VMEM((blocks * 2 * ext * 8, height), f32),
             pltpu.SMEM((bits,), jnp.int32),
             pltpu.SMEM((bits,), jnp.int32),
             pltpu.SMEM((bits * CAP,), jnp.int32),
-            pltpu.SemaphoreType.DMA((2, blocks)),
-            pltpu.SemaphoreType.DMA((2,)),
         ],
         compiler_params=params,
+        cost_estimate=pl.CostEstimate(flops=0, bytes_accessed=2 * MIB, transcendentals=0),
         name="pack",
-    )(*(in_hbm(x) for x in (jnp.transpose(block_links, (2, 0, 1)), flat_node, mode_shapes, fraction, velocity)))
-    outgoing, (red, got, fill, vel) = packed[:bits], packed[bits:]
-    received = [None] * bits
-    for k in reversed(range(bits)):
-        received[k] = swapped(outgoing[k], "family", k)
-    is_top = lax.broadcasted_iota(jnp.int32, red.shape, 1) == modes // 8
+    )(jnp.transpose(block_links, (2, 0, 1)), fill, vel)
+    outgoing, (got, top_at) = packed[:bits], packed[bits:]
+    received = [crossed(outgoing[k], "family", 1 << k) for k in range(bits)]
+    marks = [(lax.broadcasted_iota(jnp.int32, red.shape, 1) == modes // 8).astype(f32)] * bits
+    marks[1] = top_at
     for k in range(bits):
-        other = swapped(red, "family", k)
-        red = jnp.where(is_top, jnp.maximum(red, other), red + other)
-    cells, flow = shift_tables(height)
+        other = crossed(red, "family", 1 << k)
+        red = jnp.where(marks[k] > 0.0, jnp.maximum(red, other), red + other)
     base, rate, rim, top = pl.pallas_call(
         functools.partial(rates_kernel, dims),
         out_shape=[
@@ -425,25 +438,34 @@
             pltpu.VMEM((ext, ext, height), f32),
         ],
         compiler_params=params,
-        cost_estimate=pl.CostEstimate(flops=80 * fraction.size, bytes_accessed=20 * fraction.size, transcendentals=0),
+        cost_estimate=pl.CostEstimate(flops=80 * fraction.size, bytes_accessed=RATES_BYTES, transcendentals=0),
         name="rates",
-    )(jnp.asarray(cells, jnp.bfloat16), jnp.asarray(flow, jnp.bfloat16), fill, vel, fraction_start, interface_flags)
-    updated, deck = pl.pallas_call(
-        functools.partial(final_kernel, dims, devices),
+    )(*tables, fill, vel, fraction_start, interface_flags)
+    part, deck, step = pl.pallas_call(
+        functools.partial(update_kernel, dims, devices),
         out_shape=[
-            jax.ShapeDtypeStruct(fraction.shape, f32),
+            pltpu.VMEM(fraction.shape, f32),
             jax.ShapeDtypeStruct((blocks * ext, ext), f32),
-        ],
-        in_specs=[smem] + [vmem] * (8 + bits),
+            pltpu.VMEM((8, LANES), f32),
+        ],
+        in_specs=[vmem] * 7,
+        out_specs=[vmem] * 3,
+        compiler_params=params,
+        name="update",
+    )(mobility.reshape(1, modes), flat_node, mode_shapes, red, base, rate, top)
+    updated, _ = pl.pallas_call(
+        functools.partial(final_kernel, dims),
+        out_shape=[jax.ShapeDtypeStruct(fraction.shape, f32), pltpu.VMEM(fraction.shape, f32)],
+        in_specs=[smem] + [vmem] * (3 + bits),
         out_specs=[hbm, vmem],
         scratch_shapes=[
             pltpu.VMEM((faces, 3, ext, height), f32),
-            pltpu.VMEM((blocks, ext, ext, height), f32),
             pltpu.SemaphoreType.DMA((blocks,)),
         ],
+        input_output_aliases={3: 1},
         compiler_params=params,
         name="finish",
-    )(got, mobility.reshape(1, modes), flat_node, mode_shapes, red, base, rate, rim, top, *received)
+    )(got, step, rim, part, *received)
     return updated, deck.reshape(blocks, ext, ext)
 
 

time: 30.4 us -> 28.9 us (0.951)
  the two profiles are of different devices: /device:TPU:0 before, /device:TPU:24 now
where the time goes in v3:
time: 28.9 us; the launch traced here: 28.8 us
  Pallas kernels  14.9 us (52%)
  starting transfers between devices  8.13 us (28%)
  waiting for transfers between devices  4.96 us (17%)
  between operations  0.75 us (3%)
    ppermute x8, starting transfers between devices, crossed(): lax.ppermute(x, axis, [(i, i ^ mask) for i in range(lax.axis_size(axis))])  8.13 us
    pallas_call x1, Pallas kernels, local(): pl.pallas_call(functools.partial(rates_kernel, dims), out_shape=[jax.Shap...  5.78 us
    ppermute x8, waiting for transfers between devices, crossed(): lax.ppermute(x, axis, [(i, i ^ mask) for i in range(lax.axis_size(axis))])  4.96 us
    pallas_call x1, Pallas kernels, local(): pl.pallas_call(functools.partial(reduce_kernel, dims), out_shape=[pltpu.V...  4.04 us
    pallas_call x1, Pallas kernels, local(): pl.pallas_call(functools.partial(update_kernel, dims, devices), out_shape...  1.8 us
    pallas_call x1, Pallas kernels, local(): pl.pallas_call(functools.partial(final_kernel, dims), out_shape=[jax.Shap...  1.78 us
    pallas_call x1, Pallas kernels, local(): pl.pallas_call(functools.partial(pack_kernel, dims, modes // 8), out_shap...  1.5 us
  transfers between devices with their start and end apart: 8, of which 3 were waited for; matrix products, arithmetic and copies ran while one was open for 0% of the time, Pallas kernels for 32%

profile of v3, /device:TPU:24, one launch (start us, length us, event | category | flops | bytes accessed | tf_op | source)
XLA Modules:
  0.0 28.8 jit_solution(2014849210620205110)
XLA Ops:
  0.6 0.0 copy-start.6
  0.6 4.0 %reduce.1 = (f32[8,128]{1,0:T(8,128)S(1)}, f32[4,32,32,128]{3,2,1,0:T(8,128)S(1)}, bf16[4,3,32,32,128]{4,3,2,1,0:T(8,128)(2,1)S(1)}) custom-call(s32[128,32]{1,0:T(8,128)} %bitcast.4, f32[40,2048]{1,0:T(8,128)} %shapes_ref.1, f32[4,32,32,128]{3,2,1,0:T(8,128)} %fill_hbm.1, bf16[4,3,32,32,128]{4,3,2,1,0:T(8,128)(2,1)} %vel_hbm.1), custom_call_target="tpu_custom_call" | custom-call | tf_op jit(solution)/shard_map/reduce/pallas_call | solution.py:388
  4.7 0.1 collective-permute-start
  4.8 1.1 %collective-permute-done = f32[8,128]{1,0:T(8,128)S(1)} collective-permute-done((f32[8,128]{1,0:T(8,128)S(1)}, f32[8,128]{1,0:T(8,128)S(1)}, u32[]{:S(2)}, u32[]{:S(2)}) %collective-permute-start) | collective-permute-done | bytes 4128 | tf_op jit(solution)/shard_map/ppermute | solution.py:23
  5.9 1.5 %collective-permute-start.1 = (f32[8,128]{1,0:T(8,128)S(1)}, f32[8,128]{1,0:T(8,128)S(1)}, u32[]{:S(2)}, u32[]{:S(2)}) collective-permute-start(f32[8,128]{1,0:T(8,128)S(1)} %add_select_fusion.3), channel_id=1, source_target_pairs={{0,2},{1,3},{2,0},{3,1},{4,6},{5,7},{6,4},{7,5},{8,10},{9,11},{10,... | collective-permute-start | bytes 12296 | tf_op jit(solution)/shard_map/ppermute | solution.py:23
  7.4 0.0 copy-done.6
  7.5 0.0 copy-start.5
  7.5 1.5 %pack.1 = (f32[4,3,32,128]{3,2,1,0:T(8,128)S(1)}, f32[4,3,32,128]{3,2,1,0:T(8,128)S(1)}, f32[4,3,32,128]{3,2,1,0:T(8,128)S(1)}, f32[4,3,32,128]{3,2,1,0:T(8,128)...) custom-call(s32[3,4,4]{2,1,0:T(4,128)S(1)} %bitcast.6, f32[4,32,32,128]{3,2,1,0:T(8,128)S(1)} %get-tuple-element.19.fill, ...), custom_call_target="tpu_custom_call" | custom-call | bytes 2097152 | tf_op jit(solution)/shard_map/pack/pallas_call | solution.py:404
  9.0 0.6 %collective-permute-done.1 = f32[8,128]{1,0:T(8,128)S(1)} collective-permute-done((f32[8,128]{1,0:T(8,128)S(1)}, f32[8,128]{1,0:T(8,128)S(1)}, u32[]{:S(2)}, u32[]{:S(2)}) %collective-permute-start.1) | collective-permute-done | bytes 4128 | tf_op jit(solution)/shard_map/ppermute | solution.py:23
  9.5 0.4 %collective-permute-start.2 = (f32[8,128]{1,0:T(8,128)S(1)}, f32[8,128]{1,0:T(8,128)S(1)}, u32[]{:S(2)}, u32[]{:S(2)}) collective-permute-start(f32[8,128]{1,0:T(8,128)S(1)} %add_select_fusion.2), channel_id=1, source_target_pairs={{0,4},{1,5},{2,6},{3,7},{4,0},{5,1},{6,2},{7,3},{8,12},{9,13},{10,... | collective-permute-start | bytes 12296 | tf_op jit(solution)/shard_map/ppermute | solution.py:23
  10.0 0.0 collective-permute-start.4
  10.0 1.5 %collective-permute-start.5 = (f32[4,3,32,128]{3,2,1,0:T(8,128)S(1)}, f32[4,3,32,128]{3,2,1,0:T(8,128)S(1)}, u32[]{:S(2)}, u32[]{:S(2)}) collective-permute-start(f32[4,3,32,128]{3,2,1,0:T(8,128)S(1)} %get-tuple-element.31), channel_id=1, source_target_pairs={{0,2},{1,3},{2,0},{3,1},{4,6},{5,7},{6,4},{7,5},{8,10},{9,11},{10,... | collective-permute-start | bytes 589832 | tf_op jit(solution)/shard_map/ppermute | solution.py:23
  11.5 1.6 %collective-permute-start.6 = (f32[4,3,32,128]{3,2,1,0:T(8,128)S(1)}, f32[4,3,32,128]{3,2,1,0:T(8,128)S(1)}, u32[]{:S(2)}, u32[]{:S(2)}) collective-permute-start(f32[4,3,32,128]{3,2,1,0:T(8,128)S(1)} %get-tuple-element.32), channel_id=1, source_target_pairs={{0,4},{1,5},{2,6},{3,7},{4,0},{5,1},{6,2},{7,3},{8,12},{9,13},{10,... | collective-permute-start | bytes 589832 | tf_op jit(solution)/shard_map/ppermute | solution.py:23
  13.1 0.3 %collective-permute-start.7 = (f32[4,3,32,128]{3,2,1,0:T(8,128)S(1)}, f32[4,3,32,128]{3,2,1,0:T(8,128)S(1)}, u32[]{:S(2)}, u32[]{:S(2)}) collective-permute-start(f32[4,3,32,128]{3,2,1,0:T(8,128)S(1)} %get-tuple-element.33), channel_id=1, source_target_pairs={{0,8},{1,9},{2,10},{3,11},{4,12},{5,13},{6,14},{7,15},{8,0},{9,1},... | collective-permute-start | bytes 589832 | tf_op jit(solution)/shard_map/ppermute | solution.py:23
  13.4 0.0 collective-permute-done.2
  13.4 0.0 copy-start.3
  13.5 0.0 copy-start.7
  13.5 2.7 %collective-permute-start.3 = (f32[8,128]{1,0:T(8,128)S(1)}, f32[8,128]{1,0:T(8,128)S(1)}, u32[]{:S(2)}, u32[]{:S(2)}) collective-permute-start(f32[8,128]{1,0:T(8,128)S(1)} %add_select_fusion.1), channel_id=1, source_target_pairs={{0,8},{1,9},{2,10},{3,11},{4,12},{5,13},{6,14},{7,15},{8,0},{9,1},... | collective-permute-start | bytes 12296 | tf_op jit(solution)/shard_map/ppermute | solution.py:23
  16.1 0.0 copy-done
  16.1 0.0 copy-done.1
  16.1 0.0 copy-done.4
  16.1 0.0 copy-done.5
  16.1 5.8 %rates.1 = (f32[4,32,32,128]{3,2,1,0:T(8,128)S(1)}, f32[4,32,32,128]{3,2,1,0:T(8,128)S(1)}, f32[16,5,32,128]{3,2,1,0:T(8,128)S(1)}, f32[32,128]{1,0:T(8,128)S(1)}) custom-call(bf16[256,512]{1,0:T(8,128)(2,1)S(1)} %copy-done.4, bf16[128,128]{1,0:T(8,128)(2,1)S(1)} %copy-done.5, f32[4,32,32,128]{3,2,1,0:T(8,128)S(1)} %get-tuple-element.19.fill, ...), custom_call_target="tpu_custom_call" | custom-call | flops 41943040 | bytes 10485760 | tf_op jit(solution)/shard_map/rates/pallas_call | solution.py:426
  21.9 3.3 %collective-permute-done.3 = f32[8,128]{1,0:T(8,128)S(1)} collective-permute-done((f32[8,128]{1,0:T(8,128)S(1)}, f32[8,128]{1,0:T(8,128)S(1)}, u32[]{:S(2)}, u32[]{:S(2)}) %collective-permute-start.3) | collective-permute-done | bytes 4128 | tf_op jit(solution)/shard_map/ppermute | solution.py:23
  25.2 0.0 copy-done.2
  25.2 0.0 copy-done.3
  25.2 1.8 %update.1 = (f32[4,32,32,128]{3,2,1,0:T(8,128)S(1)}, f32[128,32]{1,0:T(8,128)}, f32[8,128]{1,0:T(8,128)S(1)}) custom-call(f32[1,40]{1,0:T(1,128)S(1)} %bitcast.7, s32[128,32]{1,0:T(8,128)S(1)} %bitcast.5, f32[40,2048]{1,0:T(8,128)S(1)} %copy-done.2, f32[8,128]{1,0:T(8,128)S(1)} %add_select_fusion.red_ref, f32[4,32,32,128]{3,2,1,0:T(8,128)S(1)} %get-tuple-element.24.base_ref, ...), custom_call_target="tpu_custom_call" | custom-call | tf_op jit(solution)/shard_map/update/pallas_call | solution.py:444
  27.0 0.0 collective-permute-done.4.rest_0_
  27.0 0.0 collective-permute-done.5.rest_1_
  27.0 0.0 collective-permute-done.6.rest_2_
  27.0 0.0 collective-permute-done.7.rest_3_
  27.0 1.8 %finish.1 = (f32[4,32,32,128]{3,2,1,0:T(8,128)}, f32[4,32,32,128]{3,2,1,0:T(8,128)S(1)}) custom-call(s32[16]{0:T(128)S(4)} %get-tuple-element.21.got, f32[8,128]{1,0:T(8,128)S(1)} %get-tuple-element.27.scale_ref, f32[16,5,32,128]{3,2,1,0:T(8,128)S(1)} %get-tuple-element.28.rim_ref, ...), custom_call_target="tpu_custom_call", output_to_operand_aliasing={{1}: (3, {})} | custom-call | tf_op jit(solution)/shard_map/finish/pallas_call | solution.py:456
  (10 shorter events, 0.0 us)
Async XLA Ops:
  0.6 6.8 %copy-start.6 = (s32[4,4,3]{1,0,2:T(4,128)S(1)}, s32[4,4,3]{1,0,2:T(4,128)}, u32[]{:S(2)}) copy-start(s32[4,4,3]{1,0,2:T(4,128)} %param.14) | copy-start | bytes 580
  4.7 1.2 %collective-permute-start = (f32[8,128]{1,0:T(8,128)S(1)}, f32[8,128]{1,0:T(8,128)S(1)}, u32[]{:S(2)}, u32[]{:S(2)}) collective-permute-start(f32[8,128]{1,0:T(8,128)S(1)} %get-tuple-element.23), channel_id=1, source_target_pairs={{0,1},{1,0},{2,3},{3,2},{4,5},{5,4},{6,7},{7,6},{8,9},{9,8},{10,11... | collective-permute-start | bytes 12296 | tf_op jit(solution)/shard_map/ppermute | solution.py:23
  5.9 3.6 %collective-permute-start.1 = (f32[8,128]{1,0:T(8,128)S(1)}, f32[8,128]{1,0:T(8,128)S(1)}, u32[]{:S(2)}, u32[]{:S(2)}) collective-permute-start(f32[8,128]{1,0:T(8,128)S(1)} %add_select_fusion.3), channel_id=1, source_target_pairs={{0,2},{1,3},{2,0},{3,1},{4,6},{5,7},{6,4},{7,5},{8,10},{9,11},{10,... | collective-permute-start | bytes 12296 | tf_op jit(solution)/shard_map/ppermute | solution.py:23
  7.5 8.7 %copy-start = (f32[4,32,32,128]{3,2,1,0:T(8,128)S(1)}, f32[4,32,32,128]{3,2,1,0:T(8,128)}, u32[]{:S(2)}) copy-start(f32[4,32,32,128]{3,2,1,0:T(8,128)} %start.1) | copy-start | bytes 6291460
  7.5 8.7 %copy-start.1 = (s32[4,32,32,128]{3,2,1,0:T(8,128)S(1)}, s32[4,32,32,128]{3,2,1,0:T(8,128)}, u32[]{:S(2)}) copy-start(s32[4,32,32,128]{3,2,1,0:T(8,128)} %flag.1) | copy-start | bytes 6291460
  7.5 8.7 %copy-start.4 = (bf16[256,512]{1,0:T(8,128)(2,1)S(1)}, bf16[256,512]{1,0:T(8,128)(2,1)}, u32[]{:S(2)}) copy-start(bf16[256,512]{1,0:T(8,128)(2,1)} %constant.8.clone.cells_ref) | copy-start | bytes 786436
  7.5 8.7 %copy-start.5 = (bf16[128,128]{1,0:T(8,128)(2,1)S(1)}, bf16[128,128]{1,0:T(8,128)(2,1)}, u32[]{:S(2)}) copy-start(bf16[128,128]{1,0:T(8,128)(2,1)} %constant.9.clone.flow_ref) | copy-start | bytes 98308
  9.5 3.9 %collective-permute-start.2 = (f32[8,128]{1,0:T(8,128)S(1)}, f32[8,128]{1,0:T(8,128)S(1)}, u32[]{:S(2)}, u32[]{:S(2)}) collective-permute-start(f32[8,128]{1,0:T(8,128)S(1)} %add_select_fusion.2), channel_id=1, source_target_pairs={{0,4},{1,5},{2,6},{3,7},{4,0},{5,1},{6,2},{7,3},{8,12},{9,13},{10,... | collective-permute-start | bytes 12296 | tf_op jit(solution)/shard_map/ppermute | solution.py:23
  10.0 17.0 %collective-permute-start.4 = (f32[4,3,32,128]{3,2,1,0:T(8,128)S(1)}, f32[4,3,32,128]{3,2,1,0:T(8,128)S(1)}, u32[]{:S(2)}, u32[]{:S(2)}) collective-permute-start(f32[4,3,32,128]{3,2,1,0:T(8,128)S(1)} %get-tuple-element.30), channel_id=1, source_target_pairs={{0,1},{1,0},{2,3},{3,2},{4,5},{5,4},{6,7},{7,6},{8,9},{9,8},{10,11... | collective-permute-start | bytes 589832 | tf_op jit(solution)/shard_map/ppermute | solution.py:23
  10.0 17.0 %collective-permute-start.5 = (f32[4,3,32,128]{3,2,1,0:T(8,128)S(1)}, f32[4,3,32,128]{3,2,1,0:T(8,128)S(1)}, u32[]{:S(2)}, u32[]{:S(2)}) collective-permute-start(f32[4,3,32,128]{3,2,1,0:T(8,128)S(1)} %get-tuple-element.31), channel_id=1, source_target_pairs={{0,2},{1,3},{2,0},{3,1},{4,6},{5,7},{6,4},{7,5},{8,10},{9,11},{10,... | collective-permute-start | bytes 589832 | tf_op jit(solution)/shard_map/ppermute | solution.py:23
  11.5 15.5 %collective-permute-start.6 = (f32[4,3,32,128]{3,2,1,0:T(8,128)S(1)}, f32[4,3,32,128]{3,2,1,0:T(8,128)S(1)}, u32[]{:S(2)}, u32[]{:S(2)}) collective-permute-start(f32[4,3,32,128]{3,2,1,0:T(8,128)S(1)} %get-tuple-element.32), channel_id=1, source_target_pairs={{0,4},{1,5},{2,6},{3,7},{4,0},{5,1},{6,2},{7,3},{8,12},{9,13},{10,... | collective-permute-start | bytes 589832 | tf_op jit(solution)/shard_map/ppermute | solution.py:23
  13.1 13.9 %collective-permute-start.7 = (f32[4,3,32,128]{3,2,1,0:T(8,128)S(1)}, f32[4,3,32,128]{3,2,1,0:T(8,128)S(1)}, u32[]{:S(2)}, u32[]{:S(2)}) collective-permute-start(f32[4,3,32,128]{3,2,1,0:T(8,128)S(1)} %get-tuple-element.33), channel_id=1, source_target_pairs={{0,8},{1,9},{2,10},{3,11},{4,12},{5,13},{6,14},{7,15},{8,0},{9,1},... | collective-permute-start | bytes 589832 | tf_op jit(solution)/shard_map/ppermute | solution.py:23
  13.4 11.8 %copy-start.2 = (f32[40,2048]{1,0:T(8,128)S(1)}, f32[40,2048]{1,0:T(8,128)}, u32[]{:S(2)}) copy-start(f32[40,2048]{1,0:T(8,128)} %shapes_ref.1) | copy-start | bytes 983044
  13.4 11.7 %copy-start.3 = (s32[4,32,32]{2,1,0:T(8,128)S(1)}, s32[4,32,32]{2,1,0:T(8,128)}, u32[]{:S(2)}) copy-start(s32[4,32,32]{2,1,0:T(8,128)} %param.15) | copy-start | bytes 49156
  13.5 11.7 %copy-start.7 = (f32[40]{0:T(128)S(1)}, f32[40]{0:T(128)}, u32[]{:S(2)}) copy-start(f32[40]{0:T(128)} %param.17) | copy-start | bytes 484
  13.5 11.7 %collective-permute-start.3 = (f32[8,128]{1,0:T(8,128)S(1)}, f32[8,128]{1,0:T(8,128)S(1)}, u32[]{:S(2)}, u32[]{:S(2)}) collective-permute-start(f32[8,128]{1,0:T(8,128)S(1)} %add_select_fusion.1), channel_id=1, source_target_pairs={{0,8},{1,9},{2,10},{3,11},{4,12},{5,13},{6,14},{7,15},{8,0},{9,1},... | collective-permute-start | bytes 12296 | tf_op jit(solution)/shard_map/ppermute | solution.py:23

commit v4 on v3

--- a/solution.py
+++ b/solution.py
@@ -317,7 +317,7 @@
 
 def final_kernel(dims, got, scale_ref, rim_ref, part_in, *rest):
     blocks, ext, height, bits = dims
-    ghosts = rest[:bits]
+    ghosts = rest[:bits][::-1]
     out_hbm, part, ghost, sems = rest[bits:]
     area = ext * ext
     turned = 7 - lax.broadcasted_iota(jnp.int32, (8, height), 0)
@@ -420,9 +420,10 @@
     received = [crossed(outgoing[k], "family", 1 << k) for k in range(bits)]
     marks = [(lax.broadcasted_iota(jnp.int32, red.shape, 1) == modes // 8).astype(f32)] * bits
     marks[1] = top_at
-    for k in range(bits):
+    order = [0, 3, 2, 1] if bits == 4 else list(range(bits))
+    for q, k in enumerate(order):
         other = crossed(red, "family", 1 << k)
-        red = jnp.where(marks[k] > 0.0, jnp.maximum(red, other), red + other)
+        red = jnp.where(marks[q] > 0.0, jnp.maximum(red, other), red + other)
     base, rate, rim, top = pl.pallas_call(
         functools.partial(rates_kernel, dims),
         out_shape=[
@@ -465,7 +466,7 @@
         input_output_aliases={3: 1},
         compiler_params=params,
         name="finish",
-    )(got, step, rim, part, *received)
+    )(got, step, rim, part, *received[::-1])
     return updated, deck.reshape(blocks, ext, ext)
 
 

time: 28.9 us -> 28.2 us (0.976)
  the two profiles are of different devices: /device:TPU:24 before, /device:TPU:0 now
where the time goes in v4:
time: 28.2 us; the launch traced here: 28.1 us
  Pallas kernels  14.9 us (53%)
  starting transfers between devices  11.5 us (41%)
  waiting for transfers between devices  0.88 us (3%)
  between operations  0.76 us (3%)
    ppermute x8, starting transfers between devices, crossed(): lax.ppermute(x, axis, [(i, i ^ mask) for i in range(lax.axis_size(axis))])  11.5 us
    pallas_call x1, Pallas kernels, local(): pl.pallas_call(functools.partial(rates_kernel, dims), out_shape=[jax.Shap...  5.77 us
    pallas_call x1, Pallas kernels, local(): pl.pallas_call(functools.partial(reduce_kernel, dims), out_shape=[pltpu.V...  4.04 us
    pallas_call x1, Pallas kernels, local(): pl.pallas_call(functools.partial(update_kernel, dims, devices), out_shape...  1.8 us
    pallas_call x1, Pallas kernels, local(): pl.pallas_call(functools.partial(final_kernel, dims), out_shape=[jax.Shap...  1.78 us
    pallas_call x1, Pallas kernels, local(): pl.pallas_call(functools.partial(pack_kernel, dims, modes // 8), out_shap...  1.51 us
    ppermute x8, waiting for transfers between devices, crossed(): lax.ppermute(x, axis, [(i, i ^ mask) for i in range(lax.axis_size(axis))])  0.88 us
  transfers between devices with their start and end apart: 8, of which 1 were waited for; matrix products, arithmetic and copies ran while one was open for 0% of the time, Pallas kernels for 32%

profile of v4, /device:TPU:0, one launch (start us, length us, event | category | flops | bytes accessed | tf_op | source)
XLA Modules:
  0.0 28.1 jit_solution(9226445330356982110)
XLA Ops:
  0.6 0.0 copy-start.6
  0.6 4.0 %reduce.1 = (f32[8,128]{1,0:T(8,128)S(1)}, f32[4,32,32,128]{3,2,1,0:T(8,128)S(1)}, bf16[4,3,32,32,128]{4,3,2,1,0:T(8,128)(2,1)S(1)}) custom-call(s32[128,32]{1,0:T(8,128)} %bitcast.4, f32[40,2048]{1,0:T(8,128)} %shapes_ref.1, f32[4,32,32,128]{3,2,1,0:T(8,128)} %fill_hbm.1, bf16[4,3,32,32,128]{4,3,2,1,0:T(8,128)(2,1)} %vel_hbm.1), custom_call_target="tpu_custom_call" | custom-call | tf_op jit(solution)/shard_map/reduce/pallas_call | solution.py:388
  4.7 0.5 %collective-permute-start = (f32[8,128]{1,0:T(8,128)S(1)}, f32[8,128]{1,0:T(8,128)S(1)}, u32[]{:S(2)}, u32[]{:S(2)}) collective-permute-start(f32[8,128]{1,0:T(8,128)S(1)} %get-tuple-element.23), channel_id=1, source_target_pairs={{0,1},{1,0},{2,3},{3,2},{4,5},{5,4},{6,7},{7,6},{8,9},{9,8},{10,11... | collective-permute-start | bytes 12296 | tf_op jit(solution)/shard_map/ppermute | solution.py:23
  5.2 0.8 %collective-permute-done = f32[8,128]{1,0:T(8,128)S(1)} collective-permute-done((f32[8,128]{1,0:T(8,128)S(1)}, f32[8,128]{1,0:T(8,128)S(1)}, u32[]{:S(2)}, u32[]{:S(2)}) %collective-permute-start) | collective-permute-done | bytes 4128 | tf_op jit(solution)/shard_map/ppermute | solution.py:23
  6.0 3.9 %collective-permute-start.1 = (f32[8,128]{1,0:T(8,128)S(1)}, f32[8,128]{1,0:T(8,128)S(1)}, u32[]{:S(2)}, u32[]{:S(2)}) collective-permute-start(f32[8,128]{1,0:T(8,128)S(1)} %add_select_fusion.3), channel_id=1, source_target_pairs={{0,8},{1,9},{2,10},{3,11},{4,12},{5,13},{6,14},{7,15},{8,0},{9,1},... | collective-permute-start | bytes 12296 | tf_op jit(solution)/shard_map/ppermute | solution.py:23
  10.0 0.0 copy-done.6
  10.0 0.0 copy-start.5
  10.0 1.5 %pack.1 = (f32[4,3,32,128]{3,2,1,0:T(8,128)S(1)}, f32[4,3,32,128]{3,2,1,0:T(8,128)S(1)}, f32[4,3,32,128]{3,2,1,0:T(8,128)S(1)}, f32[4,3,32,128]{3,2,1,0:T(8,128)...) custom-call(s32[3,4,4]{2,1,0:T(4,128)S(1)} %bitcast.6, f32[4,32,32,128]{3,2,1,0:T(8,128)S(1)} %get-tuple-element.19.fill, ...), custom_call_target="tpu_custom_call" | custom-call | bytes 2097152 | tf_op jit(solution)/shard_map/pack/pallas_call | solution.py:404
  11.5 0.0 collective-permute-done.1
  11.6 1.9 %collective-permute-start.2 = (f32[8,128]{1,0:T(8,128)S(1)}, f32[8,128]{1,0:T(8,128)S(1)}, u32[]{:S(2)}, u32[]{:S(2)}) collective-permute-start(f32[8,128]{1,0:T(8,128)S(1)} %add_select_fusion.2), channel_id=1, source_target_pairs={{0,4},{1,5},{2,6},{3,7},{4,0},{5,1},{6,2},{7,3},{8,12},{9,13},{10,... | collective-permute-start | bytes 12296 | tf_op jit(solution)/shard_map/ppermute | solution.py:23
  13.5 2.6 %collective-permute-start.4 = (f32[4,3,32,128]{3,2,1,0:T(8,128)S(1)}, f32[4,3,32,128]{3,2,1,0:T(8,128)S(1)}, u32[]{:S(2)}, u32[]{:S(2)}) collective-permute-start(f32[4,3,32,128]{3,2,1,0:T(8,128)S(1)} %get-tuple-element.30), channel_id=1, source_target_pairs={{0,8},{1,9},{2,10},{3,11},{4,12},{5,13},{6,14},{7,15},{8,0},{9,1},... | collective-permute-start | bytes 589832 | tf_op jit(solution)/shard_map/ppermute | solution.py:23
  16.1 0.4 %collective-permute-start.5 = (f32[4,3,32,128]{3,2,1,0:T(8,128)S(1)}, f32[4,3,32,128]{3,2,1,0:T(8,128)S(1)}, u32[]{:S(2)}, u32[]{:S(2)}) collective-permute-start(f32[4,3,32,128]{3,2,1,0:T(8,128)S(1)} %get-tuple-element.31), channel_id=1, source_target_pairs={{0,4},{1,5},{2,6},{3,7},{4,0},{5,1},{6,2},{7,3},{8,12},{9,13},{10,... | collective-permute-start | bytes 589832 | tf_op jit(solution)/shard_map/ppermute | solution.py:23
  16.5 1.5 %collective-permute-start.6 = (f32[4,3,32,128]{3,2,1,0:T(8,128)S(1)}, f32[4,3,32,128]{3,2,1,0:T(8,128)S(1)}, u32[]{:S(2)}, u32[]{:S(2)}) collective-permute-start(f32[4,3,32,128]{3,2,1,0:T(8,128)S(1)} %get-tuple-element.32), channel_id=1, source_target_pairs={{0,2},{1,3},{2,0},{3,1},{4,6},{5,7},{6,4},{7,5},{8,10},{9,11},{10,... | collective-permute-start | bytes 589832 | tf_op jit(solution)/shard_map/ppermute | solution.py:23
  18.0 0.0 collective-permute-start.7
  18.0 0.0 collective-permute-done.2
  18.0 0.0 copy-start.2
  18.0 0.0 copy-start.3
  18.1 0.0 copy-start.7
  18.1 0.6 %collective-permute-start.3 = (f32[8,128]{1,0:T(8,128)S(1)}, f32[8,128]{1,0:T(8,128)S(1)}, u32[]{:S(2)}, u32[]{:S(2)}) collective-permute-start(f32[8,128]{1,0:T(8,128)S(1)} %add_select_fusion.1), channel_id=1, source_target_pairs={{0,2},{1,3},{2,0},{3,1},{4,6},{5,7},{6,4},{7,5},{8,10},{9,11},{10,... | collective-permute-start | bytes 12296 | tf_op jit(solution)/shard_map/ppermute | solution.py:23
  18.6 0.0 copy-done
  18.7 0.0 copy-done.4
  18.7 5.8 %rates.1 = (f32[4,32,32,128]{3,2,1,0:T(8,128)S(1)}, f32[4,32,32,128]{3,2,1,0:T(8,128)S(1)}, f32[16,5,32,128]{3,2,1,0:T(8,128)S(1)}, f32[32,128]{1,0:T(8,128)S(1)}) custom-call(bf16[256,512]{1,0:T(8,128)(2,1)S(1)} %copy-done.4, bf16[128,128]{1,0:T(8,128)(2,1)S(1)} %copy-done.5, f32[4,32,32,128]{3,2,1,0:T(8,128)S(1)} %get-tuple-element.19.fill, ...), custom_call_target="tpu_custom_call" | custom-call | flops 41943040 | bytes 10485760 | tf_op jit(solution)/shard_map/rates/pallas_call | solution.py:427
  24.4 0.0 collective-permute-done.3
  24.5 0.0 copy-done.2
  24.5 0.0 copy-done.3
  24.5 0.0 copy-done.7
  24.5 1.8 %update.1 = (f32[4,32,32,128]{3,2,1,0:T(8,128)S(1)}, f32[128,32]{1,0:T(8,128)}, f32[8,128]{1,0:T(8,128)S(1)}) custom-call(f32[1,40]{1,0:T(1,128)S(1)} %bitcast.7, s32[128,32]{1,0:T(8,128)S(1)} %bitcast.5, f32[40,2048]{1,0:T(8,128)S(1)} %copy-done.2, f32[8,128]{1,0:T(8,128)S(1)} %add_select_fusion.red_ref, f32[4,32,32,128]{3,2,1,0:T(8,128)S(1)} %get-tuple-element.24.base_ref, ...), custom_call_target="tpu_custom_call" | custom-call | tf_op jit(solution)/shard_map/update/pallas_call | solution.py:445
  26.3 0.0 collective-permute-done.4.rest_0_
  26.3 0.0 collective-permute-done.5.rest_1_
  26.3 0.0 collective-permute-done.6.rest_2_
  26.3 0.0 collective-permute-done.7.rest_3_
  26.3 1.8 %finish.1 = (f32[4,32,32,128]{3,2,1,0:T(8,128)}, f32[4,32,32,128]{3,2,1,0:T(8,128)S(1)}) custom-call(s32[16]{0:T(128)S(4)} %get-tuple-element.21.got, f32[8,128]{1,0:T(8,128)S(1)} %get-tuple-element.27.scale_ref, f32[16,5,32,128]{3,2,1,0:T(8,128)S(1)} %get-tuple-element.28.rim_ref, ...), custom_call_target="tpu_custom_call", output_to_operand_aliasing={{1}: (3, {})} | custom-call | tf_op jit(solution)/shard_map/finish/pallas_call | solution.py:457
  (10 shorter events, 0.0 us)
Async XLA Ops:
  0.6 9.3 %copy-start.6 = (s32[4,4,3]{1,0,2:T(4,128)S(1)}, s32[4,4,3]{1,0,2:T(4,128)}, u32[]{:S(2)}) copy-start(s32[4,4,3]{1,0,2:T(4,128)} %param.14) | copy-start | bytes 580
  4.7 1.3 %collective-permute-start = (f32[8,128]{1,0:T(8,128)S(1)}, f32[8,128]{1,0:T(8,128)S(1)}, u32[]{:S(2)}, u32[]{:S(2)}) collective-permute-start(f32[8,128]{1,0:T(8,128)S(1)} %get-tuple-element.23), channel_id=1, source_target_pairs={{0,1},{1,0},{2,3},{3,2},{4,5},{5,4},{6,7},{7,6},{8,9},{9,8},{10,11... | collective-permute-start | bytes 12296 | tf_op jit(solution)/shard_map/ppermute | solution.py:23
  6.0 5.5 %collective-permute-start.1 = (f32[8,128]{1,0:T(8,128)S(1)}, f32[8,128]{1,0:T(8,128)S(1)}, u32[]{:S(2)}, u32[]{:S(2)}) collective-permute-start(f32[8,128]{1,0:T(8,128)S(1)} %add_select_fusion.3), channel_id=1, source_target_pairs={{0,8},{1,9},{2,10},{3,11},{4,12},{5,13},{6,14},{7,15},{8,0},{9,1},... | collective-permute-start | bytes 12296 | tf_op jit(solution)/shard_map/ppermute | solution.py:23
  10.0 8.7 %copy-start = (f32[4,32,32,128]{3,2,1,0:T(8,128)S(1)}, f32[4,32,32,128]{3,2,1,0:T(8,128)}, u32[]{:S(2)}) copy-start(f32[4,32,32,128]{3,2,1,0:T(8,128)} %start.1) | copy-start | bytes 6291460
  10.0 8.7 %copy-start.1 = (s32[4,32,32,128]{3,2,1,0:T(8,128)S(1)}, s32[4,32,32,128]{3,2,1,0:T(8,128)}, u32[]{:S(2)}) copy-start(s32[4,32,32,128]{3,2,1,0:T(8,128)} %flag.1) | copy-start | bytes 6291460
  10.0 8.7 %copy-start.4 = (bf16[256,512]{1,0:T(8,128)(2,1)S(1)}, bf16[256,512]{1,0:T(8,128)(2,1)}, u32[]{:S(2)}) copy-start(bf16[256,512]{1,0:T(8,128)(2,1)} %constant.8.clone.cells_ref) | copy-start | bytes 786436
  10.0 8.7 %copy-start.5 = (bf16[128,128]{1,0:T(8,128)(2,1)S(1)}, bf16[128,128]{1,0:T(8,128)(2,1)}, u32[]{:S(2)}) copy-start(bf16[128,128]{1,0:T(8,128)(2,1)} %constant.9.clone.flow_ref) | copy-start | bytes 98308
  11.6 6.5 %collective-permute-start.2 = (f32[8,128]{1,0:T(8,128)S(1)}, f32[8,128]{1,0:T(8,128)S(1)}, u32[]{:S(2)}, u32[]{:S(2)}) collective-permute-start(f32[8,128]{1,0:T(8,128)S(1)} %add_select_fusion.2), channel_id=1, source_target_pairs={{0,4},{1,5},{2,6},{3,7},{4,0},{5,1},{6,2},{7,3},{8,12},{9,13},{10,... | collective-permute-start | bytes 12296 | tf_op jit(solution)/shard_map/ppermute | solution.py:23
  13.5 12.8 %collective-permute-start.4 = (f32[4,3,32,128]{3,2,1,0:T(8,128)S(1)}, f32[4,3,32,128]{3,2,1,0:T(8,128)S(1)}, u32[]{:S(2)}, u32[]{:S(2)}) collective-permute-start(f32[4,3,32,128]{3,2,1,0:T(8,128)S(1)} %get-tuple-element.30), channel_id=1, source_target_pairs={{0,8},{1,9},{2,10},{3,11},{4,12},{5,13},{6,14},{7,15},{8,0},{9,1},... | collective-permute-start | bytes 589832 | tf_op jit(solution)/shard_map/ppermute | solution.py:23
  16.1 10.2 %collective-permute-start.5 = (f32[4,3,32,128]{3,2,1,0:T(8,128)S(1)}, f32[4,3,32,128]{3,2,1,0:T(8,128)S(1)}, u32[]{:S(2)}, u32[]{:S(2)}) collective-permute-start(f32[4,3,32,128]{3,2,1,0:T(8,128)S(1)} %get-tuple-element.31), channel_id=1, source_target_pairs={{0,4},{1,5},{2,6},{3,7},{4,0},{5,1},{6,2},{7,3},{8,12},{9,13},{10,... | collective-permute-start | bytes 589832 | tf_op jit(solution)/shard_map/ppermute | solution.py:23
  16.5 9.8 %collective-permute-start.6 = (f32[4,3,32,128]{3,2,1,0:T(8,128)S(1)}, f32[4,3,32,128]{3,2,1,0:T(8,128)S(1)}, u32[]{:S(2)}, u32[]{:S(2)}) collective-permute-start(f32[4,3,32,128]{3,2,1,0:T(8,128)S(1)} %get-tuple-element.32), channel_id=1, source_target_pairs={{0,2},{1,3},{2,0},{3,1},{4,6},{5,7},{6,4},{7,5},{8,10},{9,11},{10,... | collective-permute-start | bytes 589832 | tf_op jit(solution)/shard_map/ppermute | solution.py:23
  18.0 8.3 %collective-permute-start.7 = (f32[4,3,32,128]{3,2,1,0:T(8,128)S(1)}, f32[4,3,32,128]{3,2,1,0:T(8,128)S(1)}, u32[]{:S(2)}, u32[]{:S(2)}) collective-permute-start(f32[4,3,32,128]{3,2,1,0:T(8,128)S(1)} %get-tuple-element.33), channel_id=1, source_target_pairs={{0,1},{1,0},{2,3},{3,2},{4,5},{5,4},{6,7},{7,6},{8,9},{9,8},{10,11... | collective-permute-start | bytes 589832 | tf_op jit(solution)/shard_map/ppermute | solution.py:23
  18.0 6.4 %copy-start.2 = (f32[40,2048]{1,0:T(8,128)S(1)}, f32[40,2048]{1,0:T(8,128)}, u32[]{:S(2)}) copy-start(f32[40,2048]{1,0:T(8,128)} %shapes_ref.1) | copy-start | bytes 983044
  18.0 6.4 %copy-start.3 = (s32[4,32,32]{2,1,0:T(8,128)S(1)}, s32[4,32,32]{2,1,0:T(8,128)}, u32[]{:S(2)}) copy-start(s32[4,32,32]{2,1,0:T(8,128)} %param.15) | copy-start | bytes 49156
  18.1 6.4 %copy-start.7 = (f32[40]{0:T(128)S(1)}, f32[40]{0:T(128)}, u32[]{:S(2)}) copy-start(f32[40]{0:T(128)} %param.17) | copy-start | bytes 484
  18.1 6.4 %collective-permute-start.3 = (f32[8,128]{1,0:T(8,128)S(1)}, f32[8,128]{1,0:T(8,128)S(1)}, u32[]{:S(2)}, u32[]{:S(2)}) collective-permute-start(f32[8,128]{1,0:T(8,128)S(1)} %add_select_fusion.1), channel_id=1, source_target_pairs={{0,2},{1,3},{2,0},{3,1},{4,6},{5,7},{6,4},{7,5},{8,10},{9,11},{10,... | collective-permute-start | bytes 12296 | tf_op jit(solution)/shard_map/ppermute | solution.py:23

commit v5 on v4

--- a/solution.py
+++ b/solution.py
@@ -61,13 +61,12 @@
         got[k * CAP + rank] = 2 * face + links[2, face // 4, face % 4]
 
 
-def pack_kernel(dims, tiles, links, fill, vel, *rest):
+def pack_kernel(dims, tiles, sent, fill, vel, *rest):
     blocks, ext, height, bits = dims
     outs = rest[:bits]
-    got, top_at, edge, count, mask, sent = rest[bits:]
+    top_at, edge = rest[bits:]
     top_at[...] = (lax.broadcasted_iota(jnp.int32, top_at.shape, 1) == tiles).astype(jnp.float32)
     area = ext * ext
-    route(links, lax.axis_index("family"), blocks, bits, count, mask, sent, got)
     for b in range(blocks):
         for side in range(2):
             x = vel[b, 1, :, side * (ext - 16) : side * (ext - 16) + 16, :].astype(jnp.float32)[:, 8 * side : 8 * side + 8]
@@ -93,6 +92,12 @@
                 outs[k][s, 0] = rows[pl.ds(b * area + near, ext, stride=ext), :]
                 outs[k][s, 1] = rows[pl.ds(b * area + after, ext, stride=ext), :]
                 outs[k][s, 2] = edge[pl.ds((b * 2 + side) * ext * 8 + side * 7, ext, stride=8), :] * sign
+
+
+def route_kernel(dims, tiles, links, sent, got, top_at, count, mask):
+    blocks, ext, height, bits = dims
+    top_at[...] = (lax.broadcasted_iota(jnp.int32, top_at.shape, 1) == tiles).astype(jnp.float32)
+    route(links, lax.axis_index("family"), blocks, bits, count, mask, sent, got)
 
 
 def reduce_kernel(dims, node_hbm, shapes_hbm, fill_hbm, vel_hbm, red_ref, fill, vel, left, right, node_ref, shapes_ref, sems, late):
@@ -169,21 +174,17 @@
     cells = np.concatenate([before, step, after, nxt], 1)
     flow = nxt + eye; flow[:, -1] = 0
     return np.concatenate([cells, cells], 0), flow
-def rates_kernel(dims, cells_ref, flow_ref, fill, vel, start, flag, base_ref, rate_ref, rim_ref, top_ref, edge, lift):
-    blocks, ext, height, bits = dims
-    area = ext * ext
-    lane = lax.broadcasted_iota(jnp.int32, (ext, height), 1)
-    row = lax.broadcasted_iota(jnp.int32, (ext, height), 0)
-    open_row = (row >= 1) & (row <= ext - 3)
-    rows = fill.reshape(blocks * area, height)
+def column_kernel(dims, tiles, cells_ref, flow_ref, fill, vel, lift, top_at):
+    blocks, ext, height, bits = dims
+    top_at[...] = (lax.broadcasted_iota(jnp.int32, top_at.shape, 1) == tiles).astype(jnp.float32)
     layers = 8
     size = layers * ext
-    top = jnp.zeros((ext, height), jnp.float32)
-    def block(b, top):
-
-        def column(c, carry):
-            x = fill[b, pl.ds(c * layers, layers)].reshape(size, height)
-            u = vel[b, 2, pl.ds(c * layers, layers)].reshape(size, height)
+
+    def block(b, carry):
+        for c in range(ext // layers):
+            part = pl.ds(c * layers, layers)
+            x = fill[b, part].reshape(size, height)
+            u = vel[b, 2, part].reshape(size, height)
             high = x.astype(jnp.bfloat16)
             low = (x - high.astype(jnp.float32)).astype(jnp.bfloat16)
             y = jnp.dot(jnp.concatenate([high, low], 1), cells_ref[...], preferred_element_type=jnp.float32)
@@ -191,13 +192,24 @@
             step = y[:, height : 2 * height]
             ahead = x + limited(step, y[:, :height])
             behind = y[:, 3 * height :] - limited(step, y[:, 2 * height : 3 * height])
-            lift[pl.ds(c * layers, layers)] = (v * jnp.where(v > 0.0, ahead, behind)).reshape(layers, ext, height)
-            return carry
-
-        lax.fori_loop(0, ext // layers, column, 0, unroll=True)
+            lift[b, part] = (v * jnp.where(v > 0.0, ahead, behind)).reshape(layers, ext, height)
+        return carry
+
+    lax.fori_loop(0, blocks, block, 0)
+
+
+def rates_kernel(dims, fill, vel, lift, start, flag, base_ref, rate_ref, rim_ref, top_ref, edge):
+    blocks, ext, height, bits = dims
+    area = ext * ext
+    lane = lax.broadcasted_iota(jnp.int32, (ext, height), 1)
+    row = lax.broadcasted_iota(jnp.int32, (ext, height), 0)
+    open_row = (row >= 1) & (row <= ext - 3)
+    rows = fill.reshape(blocks * area, height)
+    top = jnp.zeros((ext, height), jnp.float32)
+    def block(b, top):
 
         def own(i, f, h):
-            flux = lift[i]
+            flux = lift[b, i]
             rate = pltpu.roll(flux, 1, 1) - flux
             step = pltpu.roll(h, ext - 1, 0) - h
             slope = limited(pltpu.roll(step, 1, 0), step)
@@ -387,7 +399,11 @@
     tables = [jnp.asarray(x, jnp.bfloat16) for x in shift_tables(height)]
     red, fill, vel = pl.pallas_call(
         functools.partial(reduce_kernel, dims),
-        out_shape=[pltpu.VMEM((8, LANES), f32), pltpu.VMEM(fraction.shape, f32), pltpu.VMEM(velocity.shape, jnp.bfloat16)],
+        out_shape=[
+            pltpu.VMEM((8, LANES), f32),
+            pltpu.VMEM(fraction.shape, f32),
+            pltpu.VMEM(velocity.shape, jnp.bfloat16),
+        ],
         in_specs=[hbm] * 4,
         out_specs=[vmem] * 3,
         scratch_shapes=[
@@ -401,26 +417,45 @@
         compiler_params=params,
         name="reduce",
     )(*(in_hbm(x) for x in (flat_node, mode_shapes, fraction, velocity)))
+    sent, got, routed_at = pl.pallas_call(
+        functools.partial(route_kernel, dims, modes // 8),
+        out_shape=[
+            pltpu.SMEM((bits * CAP,), jnp.int32),
+            pltpu.SMEM((bits * CAP,), jnp.int32),
+            pltpu.VMEM((8, LANES), f32),
+        ],
+        in_specs=[smem],
+        out_specs=[smem, smem, vmem],
+        scratch_shapes=[pltpu.SMEM((bits,), jnp.int32), pltpu.SMEM((bits,), jnp.int32)],
+        compiler_params=params,
+        name="route",
+    )(jnp.transpose(block_links, (2, 0, 1)))
     packed = pl.pallas_call(
         functools.partial(pack_kernel, dims, modes // 8),
-        out_shape=[pltpu.VMEM((CAP, 3, ext, height), f32)] * bits + [pltpu.SMEM((bits * CAP,), jnp.int32), pltpu.VMEM((8, LANES), f32)],
+        out_shape=[pltpu.VMEM((CAP, 3, ext, height), f32)] * bits + [pltpu.VMEM((8, LANES), f32)],
         in_specs=[smem, vmem, vmem],
-        out_specs=[vmem] * bits + [smem, vmem],
+        out_specs=[vmem] * bits + [vmem],
         scratch_shapes=[
             pltpu.VMEM((blocks * 2 * ext * 8, height), f32),
-            pltpu.SMEM((bits,), jnp.int32),
-            pltpu.SMEM((bits,), jnp.int32),
-            pltpu.SMEM((bits * CAP,), jnp.int32),
         ],
         compiler_params=params,
         cost_estimate=pl.CostEstimate(flops=0, bytes_accessed=2 * MIB, transcendentals=0),
         name="pack",
-    )(jnp.transpose(block_links, (2, 0, 1)), fill, vel)
-    outgoing, (got, top_at) = packed[:bits], packed[bits:]
+    )(sent, fill, vel)
+    outgoing, top_at = packed[:bits], packed[bits]
     received = [crossed(outgoing[k], "family", 1 << k) for k in range(bits)]
     marks = [(lax.broadcasted_iota(jnp.int32, red.shape, 1) == modes // 8).astype(f32)] * bits
-    marks[1] = top_at
-    order = [0, 3, 2, 1] if bits == 4 else list(range(bits))
+    lift, lift_at = pl.pallas_call(
+        functools.partial(column_kernel, dims, modes // 8),
+        out_shape=[pltpu.VMEM(fraction.shape, f32), pltpu.VMEM((8, LANES), f32)],
+        in_specs=[vmem] * 4,
+        out_specs=[vmem] * 2,
+        compiler_params=params,
+        cost_estimate=pl.CostEstimate(flops=0, bytes_accessed=2 * MIB, transcendentals=0),
+        name="column",
+    )(*tables, fill, vel)
+    marks[0], marks[1], marks[2] = routed_at, top_at, lift_at
+    order = [0, 3, 1, 2] if bits == 4 else list(range(bits))
     for q, k in enumerate(order):
         other = crossed(red, "family", 1 << k)
         red = jnp.where(marks[q] > 0.0, jnp.maximum(red, other), red + other)
@@ -432,16 +467,13 @@
             jax.ShapeDtypeStruct((faces, 5, ext, height), f32),
             jax.ShapeDtypeStruct((ext, height), f32),
         ],
-        in_specs=[vmem] * 6,
+        in_specs=[vmem] * 5,
         out_specs=[vmem] * 4,
-        scratch_shapes=[
-            pltpu.VMEM((2 * ext * 8, height), f32),
-            pltpu.VMEM((ext, ext, height), f32),
-        ],
+        scratch_shapes=[pltpu.VMEM((2 * ext * 8, height), f32)],
         compiler_params=params,
         cost_estimate=pl.CostEstimate(flops=80 * fraction.size, bytes_accessed=RATES_BYTES, transcendentals=0),
         name="rates",
-    )(*tables, fill, vel, fraction_start, interface_flags)
+    )(fill, vel, lift, fraction_start, interface_flags)
     part, deck, step = pl.pallas_call(
         functools.partial(update_kernel, dims, devices),
         out_shape=[

time: 28.2 us -> 27.5 us (0.975)
  starting transfers between devices: 11.5 us -> 8.85 us
  waiting for transfers between devices: 0.88 us -> 2.2 us
  Pallas kernels: 14.9 us -> 15.4 us
    pallas_call x0 -> x2, Pallas kernels: none -> 2.99 us  [the longest x1 2.09 us: local(): pl.pallas_call(functools.partial(column_kernel, dims, modes // 8), out_sh...]
    ppermute x8, starting transfers between devices: 11.5 us -> 8.85 us  [crossed(): lax.ppermute(x, axis, [(i, i ^ mask) for i in range(lax.axis_size(axis))])]
    pallas_call x1, Pallas kernels: 5.77 us -> 4.19 us  [local(): pl.pallas_call(functools.partial(rates_kernel, dims), out_shape=[jax.Shap...]
    ppermute x8, waiting for transfers between devices: 0.88 us -> 2.2 us  [crossed(): lax.ppermute(x, axis, [(i, i ^ mask) for i in range(lax.axis_size(axis))])]
    pallas_call x1, Pallas kernels: 1.51 us -> 0.62 us  [local(): pl.pallas_call(functools.partial(pack_kernel, dims, modes // 8), out_shap...]
  transfers between devices with their start and end apart: 8 -> 8, of which waited for: 1 -> 1; matrix products, arithmetic and copies ran while one was open for 0% -> 0% of each run, Pallas kernels for 32% -> 35%
where the time goes in v5:
time: 27.5 us; the launch traced here: 27.3 us
  Pallas kernels  15.4 us (56%)
  starting transfers between devices  8.85 us (32%)
  waiting for transfers between devices  2.2 us (8%)
  between operations  0.78 us (3%)
    ppermute x8, starting transfers between devices, crossed(): lax.ppermute(x, axis, [(i, i ^ mask) for i in range(lax.axis_size(axis))])  8.85 us
    pallas_call x1, Pallas kernels, local(): pl.pallas_call(functools.partial(rates_kernel, dims), out_shape=[jax.Shap...  4.19 us
    pallas_call x1, Pallas kernels, local(): pl.pallas_call(functools.partial(reduce_kernel, dims), out_shape=[pltpu.V...  4.04 us
    ppermute x8, waiting for transfers between devices, crossed(): lax.ppermute(x, axis, [(i, i ^ mask) for i in range(lax.axis_size(axis))])  2.2 us
    pallas_call x1, Pallas kernels, local(): pl.pallas_call(functools.partial(column_kernel, dims, modes // 8), out_sh...  2.09 us
    pallas_call x1, Pallas kernels, local(): pl.pallas_call(functools.partial(update_kernel, dims, devices), out_shape...  1.8 us
    pallas_call x1, Pallas kernels, local(): pl.pallas_call(functools.partial(final_kernel, dims), out_shape=[jax.Shap...  1.77 us
    pallas_call x1, Pallas kernels, local(): pl.pallas_call(functools.partial(route_kernel, dims, modes // 8), out_sha...  0.9 us
  transfers between devices with their start and end apart: 8, of which 1 were waited for; matrix products, arithmetic and copies ran while one was open for 0% of the time, Pallas kernels for 35%

profile of v5, /device:TPU:0, one launch (start us, length us, event | category | flops | bytes accessed | tf_op | source)
XLA Modules:
  0.0 27.3 jit_solution(4462987737797953561)
XLA Ops:
  0.6 0.0 copy-start.6
  0.6 4.0 %reduce.1 = (f32[8,128]{1,0:T(8,128)S(1)}, f32[4,32,32,128]{3,2,1,0:T(8,128)S(1)}, bf16[4,3,32,32,128]{4,3,2,1,0:T(8,128)(2,1)S(1)}) custom-call(s32[128,32]{1,0:T(8,128)} %bitcast.4, f32[40,2048]{1,0:T(8,128)} %shapes_ref.1, f32[4,32,32,128]{3,2,1,0:T(8,128)} %fill_hbm.1, bf16[4,3,32,32,128]{4,3,2,1,0:T(8,128)(2,1)} %vel_hbm.1), custom_call_target="tpu_custom_call" | custom-call | tf_op jit(solution)/shard_map/reduce/pallas_call | solution.py:400
  4.7 0.5 %collective-permute-start = (f32[8,128]{1,0:T(8,128)S(1)}, f32[8,128]{1,0:T(8,128)S(1)}, u32[]{:S(2)}, u32[]{:S(2)}) collective-permute-start(f32[8,128]{1,0:T(8,128)S(1)} %get-tuple-element.30), channel_id=1, source_target_pairs={{0,1},{1,0},{2,3},{3,2},{4,5},{5,4},{6,7},{7,6},{8,9},{9,8},{10,11... | collective-permute-start | bytes 12296 | tf_op jit(solution)/shard_map/ppermute | solution.py:23
  5.2 0.0 copy-done.6
  5.2 0.9 %route.1 = (s32[16]{0:T(128)S(4)}, s32[16]{0:T(128)S(4)}, f32[8,128]{1,0:T(8,128)S(1)}) custom-call(s32[3,4,4]{2,1,0:T(4,128)S(1)} %bitcast.6), custom_call_target="tpu_custom_call" | custom-call | tf_op jit(solution)/shard_map/route/pallas_call | solution.py:420
  6.1 0.0 collective-permute-done
  6.1 3.8 %collective-permute-start.1 = (f32[8,128]{1,0:T(8,128)S(1)}, f32[8,128]{1,0:T(8,128)S(1)}, u32[]{:S(2)}, u32[]{:S(2)}) collective-permute-start(f32[8,128]{1,0:T(8,128)S(1)} %add_select_fusion.3), channel_id=1, source_target_pairs={{0,8},{1,9},{2,10},{3,11},{4,12},{5,13},{6,14},{7,15},{8,0},{9,1},... | collective-permute-start | bytes 12296 | tf_op jit(solution)/shard_map/ppermute | solution.py:23
  10.0 0.6 %pack.1 = (f32[4,3,32,128]{3,2,1,0:T(8,128)S(1)}, f32[4,3,32,128]{3,2,1,0:T(8,128)S(1)}, f32[4,3,32,128]{3,2,1,0:T(8,128)S(1)}, f32[4,3,32,128]{3,2,1,0:T(8,128)S(1)}, f32[8,128]{1,0:T(8,128)S(1)}) custom-call(s32[16]{0:T(128)S(4)} %get-tuple-element.27.sent, f32[4,32,32,128]{3,2,1,0:T(8,128)S(1)} %get-tuple-element.24.fill, ...), custom_call_target="tpu_custom_call" | custom-call | bytes 2097152 | tf_op jit(solution)/shard_map/pack/pallas_call | solution.py:433
  10.6 0.1 collective-permute-start.4
  10.7 1.9 %collective-permute-start.5 = (f32[4,3,32,128]{3,2,1,0:T(8,128)S(1)}, f32[4,3,32,128]{3,2,1,0:T(8,128)S(1)}, u32[]{:S(2)}, u32[]{:S(2)}) collective-permute-start(f32[4,3,32,128]{3,2,1,0:T(8,128)S(1)} %get-tuple-element.39), channel_id=1, source_target_pairs={{0,4},{1,5},{2,6},{3,7},{4,0},{5,1},{6,2},{7,3},{8,12},{9,13},{10,... | collective-permute-start | bytes 589832 | tf_op jit(solution)/shard_map/ppermute | solution.py:23
  12.6 1.5 %collective-permute-start.6 = (f32[4,3,32,128]{3,2,1,0:T(8,128)S(1)}, f32[4,3,32,128]{3,2,1,0:T(8,128)S(1)}, u32[]{:S(2)}, u32[]{:S(2)}) collective-permute-start(f32[4,3,32,128]{3,2,1,0:T(8,128)S(1)} %get-tuple-element.40), channel_id=1, source_target_pairs={{0,2},{1,3},{2,0},{3,1},{4,6},{5,7},{6,4},{7,5},{8,10},{9,11},{10,... | collective-permute-start | bytes 589832 | tf_op jit(solution)/shard_map/ppermute | solution.py:23
  14.1 0.0 collective-permute-start.7
  14.1 0.0 collective-permute-done.1
  14.1 0.6 %collective-permute-start.2 = (f32[8,128]{1,0:T(8,128)S(1)}, f32[8,128]{1,0:T(8,128)S(1)}, u32[]{:S(2)}, u32[]{:S(2)}) collective-permute-start(f32[8,128]{1,0:T(8,128)S(1)} %add_select_fusion.2), channel_id=1, source_target_pairs={{0,2},{1,3},{2,0},{3,1},{4,6},{5,7},{6,4},{7,5},{8,10},{9,11},{10,... | collective-permute-start | bytes 12296 | tf_op jit(solution)/shard_map/ppermute | solution.py:23
  14.7 0.0 copy-done.4
  14.7 0.0 copy-done.5
  14.7 0.0 copy-start
  14.7 0.0 copy-start.1
  14.7 2.1 %column.1 = (f32[4,32,32,128]{3,2,1,0:T(8,128)S(1)}, f32[8,128]{1,0:T(8,128)S(1)}) custom-call(bf16[256,512]{1,0:T(8,128)(2,1)S(1)} %copy-done.4, bf16[128,128]{1,0:T(8,128)(2,1)S(1)} %copy-done.5, f32[4,32,32,128]{3,2,1,0:T(8,128)S(1)} %get-tuple-element.24.fill, bf16[4,3,32,32,128]{4,3,2,1,0:T(8,128)(2,1)S(1)} %get-tuple-element.25.vel), custom_call_target="tpu_custom_call" | custom-call | bytes 2097152 | tf_op jit(solution)/shard_map/column/pallas_call | solution.py:448
  16.8 2.2 %collective-permute-done.2 = f32[8,128]{1,0:T(8,128)S(1)} collective-permute-done((f32[8,128]{1,0:T(8,128)S(1)}, f32[8,128]{1,0:T(8,128)S(1)}, u32[]{:S(2)}, u32[]{:S(2)}) %collective-permute-start.2) | collective-permute-done | bytes 4128 | tf_op jit(solution)/shard_map/ppermute | solution.py:23
  19.0 0.5 %collective-permute-start.3 = (f32[8,128]{1,0:T(8,128)S(1)}, f32[8,128]{1,0:T(8,128)S(1)}, u32[]{:S(2)}, u32[]{:S(2)}) collective-permute-start(f32[8,128]{1,0:T(8,128)S(1)} %add_select_fusion.1), channel_id=1, source_target_pairs={{0,4},{1,5},{2,6},{3,7},{4,0},{5,1},{6,2},{7,3},{8,12},{9,13},{10,... | collective-permute-start | bytes 12296 | tf_op jit(solution)/shard_map/ppermute | solution.py:23
  19.4 0.0 copy-done
  19.5 0.0 copy-done.1
  19.5 0.0 copy-start.7
  19.5 4.2 %rates.1 = (f32[4,32,32,128]{3,2,1,0:T(8,128)S(1)}, f32[4,32,32,128]{3,2,1,0:T(8,128)S(1)}, f32[16,5,32,128]{3,2,1,0:T(8,128)S(1)}, f32[32,128]{1,0:T(8,128)S(1)}) custom-call(f32[4,32,32,128]{3,2,1,0:T(8,128)S(1)} %get-tuple-element.24.fill, bf16[4,3,32,32,128]{4,3,2,1,0:T(8,128)(2,1)S(1)} %get-tuple-element.25.vel, ...), custom_call_target="tpu_custom_call" | custom-call | flops 41943040 | bytes 10485760 | tf_op jit(solution)/shard_map/rates/pallas_call | solution.py:462
  23.7 0.0 collective-permute-done.3
  23.7 1.8 %update.1 = (f32[4,32,32,128]{3,2,1,0:T(8,128)S(1)}, f32[128,32]{1,0:T(8,128)}, f32[8,128]{1,0:T(8,128)S(1)}) custom-call(f32[1,40]{1,0:T(1,128)S(1)} %bitcast.7, s32[128,32]{1,0:T(8,128)S(1)} %bitcast.5, f32[40,2048]{1,0:T(8,128)S(1)} %copy-done.2, f32[8,128]{1,0:T(8,128)S(1)} %add_select_fusion.red_ref, f32[4,32,32,128]{3,2,1,0:T(8,128)S(1)} %get-tuple-element.32.base_ref, ...), custom_call_target="tpu_custom_call" | custom-call | tf_op jit(solution)/shard_map/update/pallas_call | solution.py:477
  25.5 0.0 collective-permute-done.4.rest_0_
  25.5 0.0 collective-permute-done.5.rest_1_
  25.5 0.0 collective-permute-done.6.rest_2_
  25.5 0.0 collective-permute-done.7.rest_3_
  25.6 1.8 %finish.1 = (f32[4,32,32,128]{3,2,1,0:T(8,128)}, f32[4,32,32,128]{3,2,1,0:T(8,128)S(1)}) custom-call(s32[16]{0:T(128)S(4)} %get-tuple-element.23.got, f32[8,128]{1,0:T(8,128)S(1)} %get-tuple-element.35.scale_ref, f32[16,5,32,128]{3,2,1,0:T(8,128)S(1)} %get-tuple-element.36.rim_ref, ...), custom_call_target="tpu_custom_call", output_to_operand_aliasing={{1}: (3, {})} | custom-call | tf_op jit(solution)/shard_map/finish/pallas_call | solution.py:489
  (12 shorter events, 0.0 us)
Async XLA Ops:
  0.6 4.6 %copy-start.6 = (s32[4,4,3]{1,0,2:T(4,128)S(1)}, s32[4,4,3]{1,0,2:T(4,128)}, u32[]{:S(2)}) copy-start(s32[4,4,3]{1,0,2:T(4,128)} %param.14) | copy-start | bytes 580
  4.7 1.4 %collective-permute-start = (f32[8,128]{1,0:T(8,128)S(1)}, f32[8,128]{1,0:T(8,128)S(1)}, u32[]{:S(2)}, u32[]{:S(2)}) collective-permute-start(f32[8,128]{1,0:T(8,128)S(1)} %get-tuple-element.30), channel_id=1, source_target_pairs={{0,1},{1,0},{2,3},{3,2},{4,5},{5,4},{6,7},{7,6},{8,9},{9,8},{10,11... | collective-permute-start | bytes 12296 | tf_op jit(solution)/shard_map/ppermute | solution.py:23
  6.1 8.0 %collective-permute-start.1 = (f32[8,128]{1,0:T(8,128)S(1)}, f32[8,128]{1,0:T(8,128)S(1)}, u32[]{:S(2)}, u32[]{:S(2)}) collective-permute-start(f32[8,128]{1,0:T(8,128)S(1)} %add_select_fusion.3), channel_id=1, source_target_pairs={{0,8},{1,9},{2,10},{3,11},{4,12},{5,13},{6,14},{7,15},{8,0},{9,1},... | collective-permute-start | bytes 12296 | tf_op jit(solution)/shard_map/ppermute | solution.py:23
  10.0 4.7 %copy-start.4 = (bf16[256,512]{1,0:T(8,128)(2,1)S(1)}, bf16[256,512]{1,0:T(8,128)(2,1)}, u32[]{:S(2)}) copy-start(bf16[256,512]{1,0:T(8,128)(2,1)} %constant.8.clone.cells_ref) | copy-start | bytes 786436
  10.0 4.7 %copy-start.5 = (bf16[128,128]{1,0:T(8,128)(2,1)S(1)}, bf16[128,128]{1,0:T(8,128)(2,1)}, u32[]{:S(2)}) copy-start(bf16[128,128]{1,0:T(8,128)(2,1)} %constant.9.clone.flow_ref) | copy-start | bytes 98308
  10.6 14.9 %collective-permute-start.4 = (f32[4,3,32,128]{3,2,1,0:T(8,128)S(1)}, f32[4,3,32,128]{3,2,1,0:T(8,128)S(1)}, u32[]{:S(2)}, u32[]{:S(2)}) collective-permute-start(f32[4,3,32,128]{3,2,1,0:T(8,128)S(1)} %get-tuple-element.38), channel_id=1, source_target_pairs={{0,8},{1,9},{2,10},{3,11},{4,12},{5,13},{6,14},{7,15},{8,0},{9,1},... | collective-permute-start | bytes 589832 | tf_op jit(solution)/shard_map/ppermute | solution.py:23
  10.7 14.8 %collective-permute-start.5 = (f32[4,3,32,128]{3,2,1,0:T(8,128)S(1)}, f32[4,3,32,128]{3,2,1,0:T(8,128)S(1)}, u32[]{:S(2)}, u32[]{:S(2)}) collective-permute-start(f32[4,3,32,128]{3,2,1,0:T(8,128)S(1)} %get-tuple-element.39), channel_id=1, source_target_pairs={{0,4},{1,5},{2,6},{3,7},{4,0},{5,1},{6,2},{7,3},{8,12},{9,13},{10,... | collective-permute-start | bytes 589832 | tf_op jit(solution)/shard_map/ppermute | solution.py:23
  12.6 13.0 %collective-permute-start.6 = (f32[4,3,32,128]{3,2,1,0:T(8,128)S(1)}, f32[4,3,32,128]{3,2,1,0:T(8,128)S(1)}, u32[]{:S(2)}, u32[]{:S(2)}) collective-permute-start(f32[4,3,32,128]{3,2,1,0:T(8,128)S(1)} %get-tuple-element.40), channel_id=1, source_target_pairs={{0,2},{1,3},{2,0},{3,1},{4,6},{5,7},{6,4},{7,5},{8,10},{9,11},{10,... | collective-permute-start | bytes 589832 | tf_op jit(solution)/shard_map/ppermute | solution.py:23
  14.1 11.4 %collective-permute-start.7 = (f32[4,3,32,128]{3,2,1,0:T(8,128)S(1)}, f32[4,3,32,128]{3,2,1,0:T(8,128)S(1)}, u32[]{:S(2)}, u32[]{:S(2)}) collective-permute-start(f32[4,3,32,128]{3,2,1,0:T(8,128)S(1)} %get-tuple-element.41), channel_id=1, source_target_pairs={{0,1},{1,0},{2,3},{3,2},{4,5},{5,4},{6,7},{7,6},{8,9},{9,8},{10,11... | collective-permute-start | bytes 589832 | tf_op jit(solution)/shard_map/ppermute | solution.py:23
  14.1 4.9 %collective-permute-start.2 = (f32[8,128]{1,0:T(8,128)S(1)}, f32[8,128]{1,0:T(8,128)S(1)}, u32[]{:S(2)}, u32[]{:S(2)}) collective-permute-start(f32[8,128]{1,0:T(8,128)S(1)} %add_select_fusion.2), channel_id=1, source_target_pairs={{0,2},{1,3},{2,0},{3,1},{4,6},{5,7},{6,4},{7,5},{8,10},{9,11},{10,... | collective-permute-start | bytes 12296 | tf_op jit(solution)/shard_map/ppermute | solution.py:23
  14.7 4.8 %copy-start = (f32[4,32,32,128]{3,2,1,0:T(8,128)S(1)}, f32[4,32,32,128]{3,2,1,0:T(8,128)}, u32[]{:S(2)}) copy-start(f32[4,32,32,128]{3,2,1,0:T(8,128)} %start.1) | copy-start | bytes 6291460
  14.7 4.7 %copy-start.1 = (s32[4,32,32,128]{3,2,1,0:T(8,128)S(1)}, s32[4,32,32,128]{3,2,1,0:T(8,128)}, u32[]{:S(2)}) copy-start(s32[4,32,32,128]{3,2,1,0:T(8,128)} %flag.1) | copy-start | bytes 6291460
  19.0 4.7 %collective-permute-start.3 = (f32[8,128]{1,0:T(8,128)S(1)}, f32[8,128]{1,0:T(8,128)S(1)}, u32[]{:S(2)}, u32[]{:S(2)}) collective-permute-start(f32[8,128]{1,0:T(8,128)S(1)} %add_select_fusion.1), channel_id=1, source_target_pairs={{0,4},{1,5},{2,6},{3,7},{4,0},{5,1},{6,2},{7,3},{8,12},{9,13},{10,... | collective-permute-start | bytes 12296 | tf_op jit(solution)/shard_map/ppermute | solution.py:23
  19.5 4.2 %copy-start.2 = (f32[40,2048]{1,0:T(8,128)S(1)}, f32[40,2048]{1,0:T(8,128)}, u32[]{:S(2)}) copy-start(f32[40,2048]{1,0:T(8,128)} %shapes_ref.1) | copy-start | bytes 983044
  19.5 4.3 %copy-start.3 = (s32[4,32,32]{2,1,0:T(8,128)S(1)}, s32[4,32,32]{2,1,0:T(8,128)}, u32[]{:S(2)}) copy-start(s32[4,32,32]{2,1,0:T(8,128)} %param.15) | copy-start | bytes 49156
  19.5 4.3 %copy-start.7 = (f32[40]{0:T(128)S(1)}, f32[40]{0:T(128)}, u32[]{:S(2)}) copy-start(f32[40]{0:T(128)} %param.17) | copy-start | bytes 484
